TPU v7x, 256 devices: a whole 4x4x8 slice. The times are simulated.
256 devices in a mesh: row: 32 (over x, z), col: 8 (over y, core).
Axes of the slice: x: 4, y: 4, z: 8, core: 2. Of those that a mesh axis runs over, the one named last changes fastest.
Arguments:
- slab: float32 [6, 8192, 4, 2048], P(None, 'row', None, 'col'), may hold values from -18 to 27, as said below
Outputs:
- factored: float32 [6, 8192, 4, 2048], P(None, 'row', None, 'col')
Inputs may be any that keep to these rules, and one draw needn't show every extreme that they name: `slab`: read as a matrix, its leading 2 * 256 rows and columns, made symmetric from their lower triangle, are positive definite.
All inputs are finite; a program needn't handle non-finite values.
Results may differ from a plain program's by a relative error of at most 0.0022.
Values may be sent and summed in bfloat16 or wider, within the bound.
No kernel may reach another device: no remote copies, remote signals or barrier semaphores. Data moves between devices by JAX's collectives and lax.ppermute only.
A program may use at most 128 MiB of HBM per device.

v0:
```python
import functools
import jax
import jax.numpy as jnp
from jax import lax
from jax.experimental import pallas as pl
from jax.experimental.pallas import tpu as pltpu
from jax.sharding import Mesh
from jax.sharding import PartitionSpec as P

NB = 256
STEP = 8
HALF = 128
X, Z, Y, CORE = 4, 8, 4, 2
RBL, CBL = 6, 4
PART = RBL // 2
PLANE = ("x", "y", "core")


def times_transposed(left, right):
    return lax.dot_general(
        left, right, (((1,), (1,)), ((), ())), preferred_element_type=jnp.float32
    )


def lane_of(tile, lane):
    return jnp.broadcast_to(tile[:, lane:lane + 1], (STEP, HALF))


def row_of(tile, row):
    return jnp.broadcast_to(tile[row:row + 1, :], tile.shape)


def twice(value):
    return jnp.concatenate([value, value], axis=1)


def symmetric(value):
    rows = lax.broadcasted_iota(jnp.int32, (NB, NB), 0)
    cols = lax.broadcasted_iota(jnp.int32, (NB, NB), 1)
    return jnp.where(rows >= cols, value, value.T)


def factor(work, inverse_ref, upper_ref):
    lanes = lax.broadcasted_iota(jnp.int32, (STEP, NB), 1)
    rows = lax.broadcasted_iota(jnp.int32, (STEP, NB), 0)
    for step in range(NB // STEP):
        j = step * STEP
        half = j // HALF * HALF
        tile = work[j:j + STEP, :]
        diag = tile[:, half:half + HALF]
        cols = [lane_of(diag, j - half + k) for k in range(STEP)]
        left = [[row_of(cols[k], s) if k <= s else None for k in range(STEP)] for s in range(STEP)]
        low = [[None] * STEP for _ in range(STEP)]
        root = [None] * STEP
        inside = (lanes >= j) & (lanes < j + STEP)
        right = [
            jnp.where(inside, jnp.where(lanes == j + i, 1.0, 0.0), row_of(tile, i)) for i in range(STEP)
        ]
        solved = [None] * STEP
        for k in range(STEP):
            root[k] = lax.rsqrt(left[k][k])
            for s in range(k + 1, STEP):
                low[s][k] = left[s][k] * root[k]
            for s in range(k + 1, STEP):
                for m in range(k + 1, s + 1):
                    left[s][m] = left[s][m] - low[s][k] * low[m][k]
            solved[k] = right[k] * twice(root[k])
            for s in range(k + 1, STEP):
                right[s] = right[s] - twice(low[s][k]) * solved[k]
        weights = [None] * STEP
        for i in range(STEP - 1, -1, -1):
            total = solved[i]
            for s in range(i + 1, STEP):
                total = total - twice(low[s][i]) * weights[s]
            weights[i] = total * twice(root[i])
        for t in range(step + 1, NB // STEP):
            other = work[t * STEP:(t + 1) * STEP, :]
            side = other[:, half:half + HALF]
            total = jnp.where(inside, 0.0, other)
            for i in range(STEP):
                total = total - twice(lane_of(side, j - half + i)) * weights[i]
            work[t * STEP:(t + 1) * STEP, :] = total
        final = solved[0]
        for i in range(1, STEP):
            final = jnp.where(rows == i, solved[i], final)
        block = jnp.zeros((STEP, NB), jnp.float32)
        for i in range(STEP):
            for s in range(i, STEP):
                value = low[s][i] if s > i else left[i][i] * root[i]
                block = jnp.where((rows == i) & (lanes == j + s), twice(value), block)
        inverse_ref[j:j + STEP, :] = jnp.where(lanes < j + STEP, final, 0.0)
        upper_ref[j:j + STEP, :] = jnp.where(lanes >= j + STEP, final, block)


def split(value):
    high = value.astype(jnp.bfloat16)
    rest = value - high.astype(jnp.float32)
    middle = rest.astype(jnp.bfloat16)
    return high, middle, (rest - middle.astype(jnp.float32)).astype(jnp.bfloat16)


def times_table(value, table):
    high, middle, low = split(value)
    wide = jnp.concatenate([high, high, high, middle, middle, low], axis=1)
    return jnp.dot(wide, table, preferred_element_type=jnp.float32)


def leading_kernel(pieces, tables, lower, first_low, source, inverse, upper, work):
    for part in range(2):
        source[part] = pieces[:, 2 * part].reshape(NB, NB)

    @pl.loop(0, 2)
    def _(panel):
        work[...] = symmetric(source[panel])
        factor(work, inverse, upper)
        lower[panel] = upper[...].T
        high, middle, low = split(inverse[...].T)
        for place, term in enumerate([high, middle, low, high, middle, high]):
            tables[panel, place * NB:(place + 1) * NB, :] = term

        @pl.when(panel == 0)
        def _():
            rows = times_table(pieces[:, 1].reshape(NB, NB), tables[0]).astype(jnp.bfloat16)
            first_low[...] = rows.T
            source[1] = source[1] - times_transposed(rows, rows)


def factor_leading(pieces):
    whole = pl.BlockSpec(memory_space=pltpu.VMEM)
    square = pltpu.VMEM((NB, NB), jnp.float32)
    return pl.pallas_call(
        leading_kernel,
        out_shape=[
            jax.ShapeDtypeStruct((2, 6 * NB, NB), jnp.bfloat16),
            jax.ShapeDtypeStruct((2, NB, NB), jnp.float32),
            jax.ShapeDtypeStruct((NB, NB), jnp.bfloat16),
        ],
        in_specs=[whole],
        out_specs=[whole] * 3,
        scratch_shapes=[pltpu.VMEM((2, NB, NB), jnp.float32), square, square, square],
        compiler_params=pltpu.CompilerParams(vmem_limit_bytes=32 * 2**20),
        cost_estimate=pl.CostEstimate(flops=2**10, bytes_accessed=2**10, transcendentals=0),
        name="leading",
    )(pieces)


def panel_rows(raw_first, raw_second, tables, first_low):
    first = times_table(raw_first, tables[0])
    first_bf16 = first.astype(jnp.bfloat16)
    column = raw_second - jnp.dot(first_bf16, first_low[...], preferred_element_type=jnp.float32)
    second = times_table(column, tables[1])
    return first, first_bf16, second


def left_kernel(index, mine_low, other_low, mine_high, other_high, tables, lower, first_low, both, lead):
    step = pl.program_id(0)
    swap = index[1] % CORE == 1
    mine = jnp.concatenate([mine_low[0], mine_high[0]])
    other = jnp.concatenate([other_low[0], other_high[0]])
    raw_first = jnp.where(swap, other, mine)
    raw_second = jnp.where(swap, mine, other)
    first, first_bf16, second = panel_rows(raw_first, raw_second, tables, first_low)
    for part in range(2):
        row_block = (part * PART + step) * (X * Z) + index[0]
        rows = slice(part * NB, (part + 1) * NB)
        one, two, one_bf16 = first[rows], second[rows], first_bf16[rows]
        if part == 0:
            one = jnp.where(row_block == 0, lower[0], one)
            one_bf16 = one.astype(jnp.bfloat16)
            two = jnp.where(row_block == 1, lower[1], jnp.where(row_block == 0, 0.0, two))
        both[part, 0, :, :NB] = one_bf16
        both[part, 0, :, NB:] = two.astype(jnp.bfloat16)
        lead[part, 0] = jnp.where(swap, two, one)


def fixed(*shape):
    return pl.BlockSpec(shape, lambda b, _: (0,) * len(shape))


def by_row(*shape):
    return pl.BlockSpec((1,) + shape, lambda b, _: (b,) + (0,) * len(shape))


def left_rows(index, mine_low, other_low, mine_high, other_high, tables, lower, first_low):
    pair = lambda *shape: pl.BlockSpec((2, 1) + shape, lambda b, _: (0, b) + (0,) * len(shape))
    return pl.pallas_call(
        left_kernel,
        grid_spec=pltpu.PrefetchScalarGridSpec(
            num_scalar_prefetch=1,
            grid=(PART,),
            in_specs=[by_row(NB, NB)] * 4 + [fixed(2, 6 * NB, NB), fixed(2, NB, NB), fixed(NB, NB)],
            out_specs=[pair(NB, 2 * NB), pair(NB, NB)],
        ),
        out_shape=[
            jax.ShapeDtypeStruct((2, PART, NB, 2 * NB), jnp.bfloat16),
            jax.ShapeDtypeStruct((2, PART, NB, NB), jnp.float32),
        ],
        compiler_params=pltpu.CompilerParams(vmem_limit_bytes=32 * 2**20),
        cost_estimate=pl.CostEstimate(flops=2**10, bytes_accessed=2**10, transcendentals=0),
        name="left_rows",
    )(index, mine_low, other_low, mine_high, other_high, tables, lower, first_low)


def update_kernel(index, slab, both, lead, raw, tables, first_low, out, right):
    row_block = pl.program_id(0) * (X * Z) + index[0]
    col_index = index[1]

    @pl.when(pl.program_id(0) == 0)
    def _():
        for m in range(CBL):
            raw_first = raw[m * Z:(m + 1) * Z, 0].reshape(NB, NB)
            raw_second = raw[m * Z:(m + 1) * Z, 1].reshape(NB, NB)
            _, first_bf16, second = panel_rows(raw_first, raw_second, tables, first_low)
            columns = slice(m * NB, (m + 1) * NB)
            right[:NB, columns] = first_bf16.T
            right[NB:, columns] = second.astype(jnp.bfloat16).T

    change = jnp.dot(both[0, 0], right[...], preferred_element_type=jnp.float32)
    for m in range(CBL):
        live = (row_block >= 2) & (m * (Y * CORE) + col_index >= 2)
        value = slab[0, :, m, :] - jnp.where(live, change[:, m * NB:(m + 1) * NB], 0.0)
        if m == 0:
            value = jnp.where(col_index < 2, lead[0, 0], value)
        out[0, :, m, :] = value


def update(index, slab, both, lead, raw, tables, first_low):
    part = lambda *shape: pl.BlockSpec(
        (1, 1) + shape, lambda b, _: (b // PART, b % PART) + (0,) * len(shape)
    )
    return pl.pallas_call(
        update_kernel,
        grid_spec=pltpu.PrefetchScalarGridSpec(
            num_scalar_prefetch=1,
            grid=(RBL,),
            in_specs=[
                by_row(NB, CBL, NB), part(NB, 2 * NB), part(NB, NB),
                fixed(X * Z, 2, NB // Z, NB), fixed(2, 6 * NB, NB), fixed(NB, NB),
            ],
            out_specs=by_row(NB, CBL, NB),
            scratch_shapes=[pltpu.VMEM((2 * NB, CBL * NB), jnp.bfloat16)],
        ),
        out_shape=jax.ShapeDtypeStruct(slab.shape, jnp.float32),
        compiler_params=pltpu.CompilerParams(vmem_limit_bytes=40 * 2**20),
        cost_estimate=pl.CostEstimate(flops=2**10, bytes_accessed=2**10, transcendentals=0),
        name="update",
    )(index, slab, both, lead, raw, tables, first_low)


def tie(value, *others):
    return lax.optimization_barrier((value,) + others)[0]


def per_device(slab):
    x, z = lax.axis_index("x"), lax.axis_index("z")
    y, core = lax.axis_index("y"), lax.axis_index("core")
    column = y * CORE + core
    index = jnp.stack([x * Z + z, column]).astype(jnp.int32)
    top = slab[0, :, 0, :]
    own_low = slab[1:PART, :, 0, :]
    own_high = slab[PART:, :, 0, :]
    chunk = NB // Z

    def place(k):
        pairs = [(zz * Y * CORE + k, zz * Y * CORE + zz) for zz in range(Z)]
        return lax.ppermute(top, ("z", "y", "core"), pairs)

    scattered = lax.all_to_all(top.reshape(X * Y * CORE, STEP, NB), PLANE, 0, 0)[:2]
    one_top = lax.ppermute(top, "y", [(0, 1)])
    three_top = lax.ppermute(top, "y", [(0, 3)])
    scattered = tie(scattered, own_low, own_high, one_top, three_top)
    placed = jnp.stack([place(0), place(1)])
    to_z = jnp.concatenate(
        [
            jnp.broadcast_to(scattered.reshape(1, 2 * STEP, NB), (Z, 2 * STEP, NB)),
            placed.reshape(2, Z, chunk, NB).transpose(1, 0, 2, 3).reshape(Z, 2 * chunk, NB),
        ],
        axis=1,
    )
    one_low = lax.ppermute(own_low, "y", [(0, 1)])
    three_low = lax.ppermute(own_low, "y", [(0, 3)])
    join = lambda first, rest: jnp.concatenate([first[None], rest])
    from_z = lax.all_to_all(to_z, "z", 0, 0)
    from_z = tie(from_z, one_low, three_low)
    own_low, one_low, three_low = join(top, own_low), join(one_top, one_low), join(three_top, three_low)
    pieces = jnp.concatenate([from_z[0, :STEP], from_z[1, :2 * STEP]]).reshape(1, 3, STEP, NB)
    one_high = lax.ppermute(own_high, "y", [(0, 1)])
    three_high = lax.ppermute(own_high, "y", [(0, 3)])
    two_low = lax.ppermute(one_low, "y", [(1, 2)])
    pieces = lax.all_to_all(
        jnp.broadcast_to(pieces, (X * Y * CORE, 3, STEP, NB)), PLANE, 0, 0
    )
    pieces = tie(pieces, one_high, three_high)
    two_high = lax.ppermute(three_high, "y", [(3, 2)])
    raw = lax.dynamic_index_in_dim(from_z[:, 2 * STEP:], column, 0).reshape(1, 2, chunk, NB)
    raw = jnp.broadcast_to(raw, (X * Z, 2, chunk, NB))
    raw = lax.all_to_all(tie(raw, pieces, one_high, three_high), ("x", "z"), 0, 0)

    tables, lower, first_low = factor_leading(pieces)

    def panel(own, one, two, three):
        mine = jnp.where(y == 0, own, jnp.where(y == 1, one, jnp.where(y == 3, three, two)))
        return mine, lax.ppermute(mine, "core", [(0, 1), (1, 0)])

    low = panel(own_low, one_low, tie(two_low, tables), three_low)
    high = panel(own_high, one_high, tie(two_high, tables), three_high)
    both, lead = left_rows(index, *low, *high, tables, lower, first_low)
    return update(index, slab, both, lead, raw, tables, first_low)


def solution(mesh):
    inner = Mesh(mesh.devices.reshape(X, Z, Y, CORE), ("x", "z", "y", "core"))
    spec = P(None, ("x", "z"), None, ("y", "core"))
    return jax.shard_map(per_device, mesh=inner, in_specs=(spec,), out_specs=spec, check_vma=False)
```

profile of v0, /device:TPU:24, one launch (start us, length us, event | category | flops | bytes accessed | tf_op | source)
XLA Modules:
  0.0 152.5 jit_solution(11795426920954979696)
XLA Ops:
  0.0 1.4 slice.21
  2.1 1.3 collective-permute-start.2
  5.5 11.2 %all-to-all-start = ((f32[32,8,256]{2,1,0:T(8,128)}), f32[32,8,256]{2,1,0:T(8,128)S(1)}, u32[]{:S(2)}, u32[]{:S(2)}) async-start(f32[32,8,256]{2,1,0:T(8,128)} %bitcast.35), calls=%async_computation | async-start | bytes 524288 | tf_op jit(solution)/shard_map/all_to_all | solution.py:268
  16.7 2.0 %slice.22 = f32[2,256,1,256]{3,2,1,0:T(1,128)S(1)} slice(f32[6,256,4,256]{3,2,1,0:T(4,128)} %slab.1), slice={[1:3], [0:256], [0:1], [0:256]} | slice | bytes 1048576 | tf_op jit(solution)/shard_map/slice | solution.py:260
  18.7 2.4 %slice.24 = f32[3,256,1,256]{3,2,1,0:T(1,128)S(1)} slice(f32[6,256,4,256]{3,2,1,0:T(4,128)} %slab.1), slice={[3:6], [0:256], [0:1], [0:256]} | slice | bytes 1572864 | tf_op jit(solution)/shard_map/slice | solution.py:261
  22.1 1.7 %all-to-all-done = f32[32,8,256]{2,1,0:T(8,128)S(1)} async-done(((f32[32,8,256]{2,1,0:T(8,128)}), f32[32,8,256]{2,1,0:T(8,128)S(1)}, u32[]{:S(2)}, u32[]{:S(2)}) %all-to-all-start) | async-done | bytes 262176 | tf_op jit(solution)/shard_map/all_to_all | solution.py:268
  24.8 6.8 %all-to-all-start.1 = ((f32[8,80,256]{2,1,0:T(8,128)}), f32[8,80,256]{2,1,0:T(8,128)S(1)}, u32[]{:S(2)}, u32[]{:S(2)}) async-start(f32[8,80,256]{2,1,0:T(8,128)} %pad_maximum_fusion.1), calls=%async_computation.1 | async-start | bytes 1310720 | tf_op jit(solution)/shard_map/all_to_all | solution.py:283
  31.6 1.3 collective-permute-start.3
  33.6 1.3 collective-permute-start.8
  34.9 1.6 %collective-permute-start.7 = (f32[3,256,256]{2,1,0:T(8,128)S(1)}, f32[3,256,256]{2,1,0:T(8,128)}, u32[]{:S(2)}, u32[]{:S(2)}) collective-permute-start(f32[3,256,256]{2,1,0:T(8,128)S(1)} %bitcast.43), channel_id=1, source_target_pairs={{0,2},{1,3},{8,10},{9,11},{16,18},{17,19},{24,26},{25,27},{32,34},... | collective-permute-start | bytes 2359304 | tf_op jit(solution)/shard_map/ppermute | solution.py:287
  36.4 13.0 %collective-permute-done.3 = f32[2,256,256]{2,1,0:T(8,128)S(1)} collective-permute-done((f32[2,256,256]{2,1,0:T(8,128)S(1)}, f32[2,256,256]{2,1,0:T(8,128)S(1)}, u32[]{:S(2)}, u32[]{:S(2)}) %collective-permute-start.3) | collective-permute-done | bytes 524320 | tf_op jit(solution)/shard_map/ppermute | solution.py:281
  49.5 3.1 %all-to-all-done.1 = f32[8,80,256]{2,1,0:T(8,128)S(1)} async-done(((f32[8,80,256]{2,1,0:T(8,128)}), f32[8,80,256]{2,1,0:T(8,128)S(1)}, u32[]{:S(2)}, u32[]{:S(2)}) %all-to-all-start.1) | async-done | bytes 655392 | tf_op jit(solution)/shard_map/all_to_all | solution.py:283
  53.5 8.0 %all-to-all-start.2 = ((f32[32,3,8,256]{3,2,1,0:T(8,128)}), f32[32,3,8,256]{3,2,1,0:T(8,128)S(1)}, u32[]{:S(2)}, u32[]{:S(2)}) async-start(f32[32,3,8,256]{3,2,1,0:T(8,128)} %broadcast_in_dim.32), calls=%async_computation.2 | async-start | bytes 1572864 | tf_op jit(solution)/shard_map/all_to_all | solution.py:290
  61.6 11.5 %collective-permute-done.8 = f32[3,256,256]{2,1,0:T(8,128)} collective-permute-done((f32[3,256,256]{2,1,0:T(8,128)S(1)}, f32[3,256,256]{2,1,0:T(8,128)}, u32[]{:S(2)}, u32[]{:S(2)}) %collective-permute-start.8) | collective-permute-done | bytes 786464 | tf_op jit(solution)/shard_map/ppermute | solution.py:288
  74.0 1.6 %broadcast_in_dim.34 = f32[32,2,32,256]{3,2,1,0:T(8,128)} broadcast(f32[2,32,256]{2,1,0:T(8,128)S(1)} %bitcast.45), dimensions={1,2,3} | broadcast | bytes 2162688 | tf_op jit(solution)/shard_map/broadcast_in_dim | solution.py:296
  75.6 8.0 %all-to-all-start.3 = ((f32[32,2,32,256]{3,2,1,0:T(8,128)}), f32[32,2,32,256]{3,2,1,0:T(8,128)S(1)}, u32[]{:S(2)}, u32[]{:S(2)}) async-start(f32[32,2,32,256]{3,2,1,0:T(8,128)} %broadcast_in_dim.34), calls=%async_computation.3 | async-start | bytes 4194304 | tf_op jit(solution)/shard_map/all_to_all | solution.py:297
  83.6 4.8 %collective-permute-start.10 = (f32[3,256,256]{2,1,0:T(8,128)}, f32[3,256,256]{2,1,0:T(8,128)}, u32[]{:S(2)}, u32[]{:S(2)}) collective-permute-start(f32[3,256,256]{2,1,0:T(8,128)} %collective-permute-done.8), channel_id=1, source_target_pairs={{6,4},{7,5},{14,12},{15,13},{22,20},{23,21},{30,28},{31,29},{38,36... | collective-permute-start | bytes 2359304 | tf_op jit(solution)/shard_map/ppermute | solution.py:294
  88.4 1.9 %pad_maximum_fusion = f32[3,256,256]{2,1,0:T(8,128)} fusion(f32[2,256,256]{2,1,0:T(8,128)S(1)} %collective-permute-done.1, f32[1,256,256]{2,1,0:T(8,128)} %bitcast.40), kind=kLoop, calls=%fused_computation.1 | loop fusion | flops 196608 | bytes 1572864 | tf_op jit(solution)/shard_map/concatenate | solution.py:282
  90.3 1.6 %collective-permute-start.4 = (f32[3,256,256]{2,1,0:T(8,128)}, f32[3,256,256]{2,1,0:T(8,128)}, u32[]{:S(2)}, u32[]{:S(2)}) collective-permute-start(f32[3,256,256]{2,1,0:T(8,128)} %pad_maximum_fusion), channel_id=1, source_target_pairs={{2,4},{3,5},{10,12},{11,13},{18,20},{19,21},{26,28},{27,29},{34,36... | collective-permute-start | bytes 2359304 | tf_op jit(solution)/shard_map/ppermute | solution.py:289
  91.9 24.4 %leading.1 = (bf16[2,1536,256]{2,1,0:T(8,128)(2,1)S(1)}, f32[2,256,256]{2,1,0:T(8,128)S(1)}, bf16[256,256]{1,0:T(8,128)(2,1)S(1)}) custom-call(f32[32,3,8,256]{3,2,1,0:T(8,128)S(1)} %all-to-all-done.2.pieces), custom_call_target="tpu_custom_call" | custom-call | flops 1024 | bytes 1024 | tf_op jit(solution)/shard_map/leading/pallas_call | solution.py:131
  116.3 2.4 %maximum_select_fusion.mine_low = f32[3,256,256]{2,1,0:T(8,128)S(1)} fusion(f32[2,256,256]{2,1,0:T(8,128)} %bitcast.38, f32[1,256,256]{2,1,0:T(8,128)} %bitcast.27.clone.2, f32[3,256,256]{2,1,0:T(8,128)} %collective-permute-done.4, f32[2,256,256]{2,1,0:T(8,128)} %copy-done.13, f32[1,256,256]{2,1,0:T(8,128)} %bitcast.44, pred[]{:T(512)S(6)} %eq.14, pred[]{:T(512)S(6)} %eq.13, ...), kind=kLoop, calls=%fused_computation | loop fusion | flops 1179648 | bytes 3932163 | tf_op jit(solution)/shard_map/jit(_where)/select_n | solution.py:302
  118.8 2.3 %select_select_fusion.mine_high = f32[3,256,256]{2,1,0:T(8,128)} fusion(f32[3,256,256]{2,1,0:T(8,128)} %collective-permute-done.7, f32[3,256,256]{2,1,0:T(8,128)} %collective-permute-done.8, f32[3,256,256]{2,1,0:T(8,128)} %collective-permute-done.10, pred[]{:T(512)S(6)} %eq.14, pred[]{:T(512)S(6)} %eq.13, pred[]{:T(512)S(6)} %eq.12, ...), kind=kLoop, calls=%fused_computation.5 | loop fusion | flops 589824 | bytes 3932163 | tf_op jit(solution)/shard_map/jit(_where)/select_n | solution.py:302
  121.7 2.2 %collective-permute-done.11.other_high = f32[3,256,256]{2,1,0:T(8,128)} collective-permute-done((f32[3,256,256]{2,1,0:T(8,128)}, f32[3,256,256]{2,1,0:T(8,128)}, u32[]{:S(2)}, u32[]{:S(2)}) %collective-permute-start.11) | collective-permute-done | bytes 786464 | tf_op jit(solution)/shard_map/ppermute | solution.py:303
  123.9 1.4 copy-done.2
  125.3 7.7 %left_rows.1 = (bf16[2,3,256,512]{3,2,1,0:T(8,128)(2,1)S(1)}, f32[2,3,256,256]{3,2,1,0:T(8,128)S(1)}) custom-call(s32[2]{0:T(128)S(1)} %pad_add_fusion.index, f32[3,256,256]{2,1,0:T(8,128)S(1)} %maximum_select_fusion.mine_low, f32[3,256,256]{2,1,0:T(8,128)} %collective-permute-done.9.other_low, f32[3,256,256]{2,1,0:T(8,128)} %select_select_fusion.mine_high, ...), custom_call_target="tpu_custom_call" | custom-call | flops 1024 | bytes 1024 | tf_op jit(solution)/shard_map/left_rows/pallas_call | solution.py:186
  132.9 1.1 copy-done.4
  134.1 1.2 copy-done.6
  135.2 2.8 %copy-done = f32[6,256,4,256]{3,2,1,0:T(4,128)S(1)} copy-done((f32[6,256,4,256]{3,2,1,0:T(4,128)S(1)}, f32[6,256,4,256]{3,2,1,0:T(4,128)}, u32[]{:S(2)}) %copy-start) | copy-done | bytes 6291480
  138.0 1.4 copy-done.3
  139.4 1.4 copy-done.5
  140.8 1.4 copy-done.7
  142.2 10.3 %update.1 = f32[6,256,4,256]{3,2,1,0:T(4,128)} custom-call(s32[2]{0:T(128)S(1)} %pad_add_fusion.index, f32[6,256,4,256]{3,2,1,0:T(4,128)S(1)} %copy-done, bf16[2,3,256,512]{3,2,1,0:T(8,128)(2,1)S(1)} %copy-done.5, f32[2,3,256,256]{3,2,1,0:T(8,128)S(1)} %copy-done.7, f32[32,2,32,256]{3,2,1,0:T(8,128)S(1)} %all-to-all-done.3.raw, ...), custom_call_target="tpu_custom_call" | custom-call | flops 1024 | bytes 1024 | tf_op jit(solution)/shard_map/update/pallas_call | solution.py:231
  (54 shorter events, 8.0 us)
Async XLA Ops:
  2.1 21.6 %collective-permute-start.2 = (f32[256,256]{1,0:T(8,128)}, f32[256,256]{1,0:T(8,128)S(1)}, u32[]{:S(2)}, u32[]{:S(2)}) collective-permute-start(f32[256,256]{1,0:T(8,128)} %bitcast.26.clone.2), channel_id=1, source_target_pairs={{0,6},{1,7},{8,14},{9,15},{16,22},{17,23},{24,30},{25,31},{32,38},... | collective-permute-start | bytes 786440 | tf_op jit(solution)/shard_map/ppermute | solution.py:270
  3.4 20.3 %collective-permute-start = (f32[256,256]{1,0:T(8,128)}, f32[256,256]{1,0:T(8,128)S(1)}, u32[]{:S(2)}, u32[]{:S(2)}) collective-permute-start(f32[256,256]{1,0:T(8,128)} %bitcast.26.clone.2), channel_id=1, source_target_pairs={{0,2},{1,3},{8,10},{9,11},{16,18},{17,19},{24,26},{25,27},{32,34},... | collective-permute-start | bytes 786440 | tf_op jit(solution)/shard_map/ppermute | solution.py:269
  4.1 19.7 %collective-permute-start.5 = (f32[256,256]{1,0:T(8,128)}, f32[256,256]{1,0:T(8,128)S(1)}, u32[]{:S(2)}, u32[]{:S(2)}) collective-permute-start(f32[256,256]{1,0:T(8,128)} %bitcast.26.clone.2), channel_id=1, source_target_pairs={{0,0},{8,9},{16,18},{24,27},{32,36},{40,45},{48,54},{56,63},{64,64... | collective-permute-start | bytes 786440 | tf_op jit(solution)/shard_map/ppermute | solution.py:266
  4.8 19.0 %collective-permute-start.6 = (f32[256,256]{1,0:T(8,128)}, f32[256,256]{1,0:T(8,128)S(1)}, u32[]{:S(2)}, u32[]{:S(2)}) collective-permute-start(f32[256,256]{1,0:T(8,128)} %bitcast.26.clone.2), channel_id=1, source_target_pairs={{1,0},{9,9},{17,18},{25,27},{33,36},{41,45},{49,54},{57,63},{65,64... | collective-permute-start | bytes 786440 | tf_op jit(solution)/shard_map/ppermute | solution.py:266
  5.5 18.3 %all-to-all-start = ((f32[32,8,256]{2,1,0:T(8,128)}), f32[32,8,256]{2,1,0:T(8,128)S(1)}, u32[]{:S(2)}, u32[]{:S(2)}) async-start(f32[32,8,256]{2,1,0:T(8,128)} %bitcast.35), calls=%async_computation | async-start | bytes 524288 | tf_op jit(solution)/shard_map/all_to_all | solution.py:268
  21.1 0.9 copy-start.8
  22.0 53.6 %copy-start.11 = (f32[2,256,1,256]{3,1,0,2:T(8,128)}, f32[2,256,1,256]{3,1,0,2:T(8,128)S(1)}, u32[]{:S(2)}) copy-start(f32[2,256,1,256]{3,1,0,2:T(8,128)S(1)} %copy.21) | copy-start | bytes 1572868
  23.8 1.0 copy-start.14
  23.8 1.0 copy-start.12
  24.8 27.8 %all-to-all-start.1 = ((f32[8,80,256]{2,1,0:T(8,128)}), f32[8,80,256]{2,1,0:T(8,128)S(1)}, u32[]{:S(2)}, u32[]{:S(2)}) async-start(f32[8,80,256]{2,1,0:T(8,128)} %pad_maximum_fusion.1), calls=%async_computation.1 | async-start | bytes 1310720 | tf_op jit(solution)/shard_map/all_to_all | solution.py:283
  31.6 17.9 %collective-permute-start.3 = (f32[2,256,256]{2,1,0:T(8,128)S(1)}, f32[2,256,256]{2,1,0:T(8,128)S(1)}, u32[]{:S(2)}, u32[]{:S(2)}) collective-permute-start(f32[2,256,256]{2,1,0:T(8,128)S(1)} %bitcast.36), channel_id=1, source_target_pairs={{0,6},{1,7},{8,14},{9,15},{16,22},{17,23},{24,30},{25,31},{32,38},... | collective-permute-start | bytes 1572872 | tf_op jit(solution)/shard_map/ppermute | solution.py:281
  32.9 16.6 %collective-permute-start.1 = (f32[2,256,256]{2,1,0:T(8,128)S(1)}, f32[2,256,256]{2,1,0:T(8,128)S(1)}, u32[]{:S(2)}, u32[]{:S(2)}) collective-permute-start(f32[2,256,256]{2,1,0:T(8,128)S(1)} %bitcast.37), channel_id=1, source_target_pairs={{0,2},{1,3},{8,10},{9,11},{16,18},{17,19},{24,26},{25,27},{32,34},... | collective-permute-start | bytes 1572872 | tf_op jit(solution)/shard_map/ppermute | solution.py:280
  33.6 39.4 %collective-permute-start.8 = (f32[3,256,256]{2,1,0:T(8,128)S(1)}, f32[3,256,256]{2,1,0:T(8,128)}, u32[]{:S(2)}, u32[]{:S(2)}) collective-permute-start(f32[3,256,256]{2,1,0:T(8,128)S(1)} %bitcast.42), channel_id=1, source_target_pairs={{0,6},{1,7},{8,14},{9,15},{16,22},{17,23},{24,30},{25,31},{32,38},... | collective-permute-start | bytes 2359304 | tf_op jit(solution)/shard_map/ppermute | solution.py:288
  34.9 38.2 %collective-permute-start.7 = (f32[3,256,256]{2,1,0:T(8,128)S(1)}, f32[3,256,256]{2,1,0:T(8,128)}, u32[]{:S(2)}, u32[]{:S(2)}) collective-permute-start(f32[3,256,256]{2,1,0:T(8,128)S(1)} %bitcast.43), channel_id=1, source_target_pairs={{0,2},{1,3},{8,10},{9,11},{16,18},{17,19},{24,26},{25,27},{32,34},... | collective-permute-start | bytes 2359304 | tf_op jit(solution)/shard_map/ppermute | solution.py:287
  49.5 4.0 %copy-start.13 = (f32[2,256,256]{2,1,0:T(8,128)}, f32[2,256,256]{2,1,0:T(8,128)S(1)}, u32[]{:S(2)}) copy-start(f32[2,256,256]{2,1,0:T(8,128)S(1)} %collective-permute-done.3) | copy-start | bytes 1572868
  49.5 38.9 %copy-start.10 = (f32[2,256,256]{2,1,0:T(8,128)}, f32[2,256,256]{2,1,0:T(8,128)S(1)}, u32[]{:S(2)}) copy-start(f32[2,256,256]{2,1,0:T(8,128)S(1)} %collective-permute-done.1) | copy-start | bytes 1572868
  53.5 20.5 %all-to-all-start.2 = ((f32[32,3,8,256]{3,2,1,0:T(8,128)}), f32[32,3,8,256]{3,2,1,0:T(8,128)S(1)}, u32[]{:S(2)}, u32[]{:S(2)}) async-start(f32[32,3,8,256]{3,2,1,0:T(8,128)} %broadcast_in_dim.32), calls=%async_computation.2 | async-start | bytes 1572864 | tf_op jit(solution)/shard_map/all_to_all | solution.py:290
  75.6 59.6 %all-to-all-start.3 = ((f32[32,2,32,256]{3,2,1,0:T(8,128)}), f32[32,2,32,256]{3,2,1,0:T(8,128)S(1)}, u32[]{:S(2)}, u32[]{:S(2)}) async-start(f32[32,2,32,256]{3,2,1,0:T(8,128)} %broadcast_in_dim.34), calls=%async_computation.3 | async-start | bytes 4194304 | tf_op jit(solution)/shard_map/all_to_all | solution.py:297
  83.6 32.7 %collective-permute-start.10 = (f32[3,256,256]{2,1,0:T(8,128)}, f32[3,256,256]{2,1,0:T(8,128)}, u32[]{:S(2)}, u32[]{:S(2)}) collective-permute-start(f32[3,256,256]{2,1,0:T(8,128)} %collective-permute-done.8), channel_id=1, source_target_pairs={{6,4},{7,5},{14,12},{15,13},{22,20},{23,21},{30,28},{31,29},{38,36... | collective-permute-start | bytes 2359304 | tf_op jit(solution)/shard_map/ppermute | solution.py:294
  90.3 26.0 %collective-permute-start.4 = (f32[3,256,256]{2,1,0:T(8,128)}, f32[3,256,256]{2,1,0:T(8,128)}, u32[]{:S(2)}, u32[]{:S(2)}) collective-permute-start(f32[3,256,256]{2,1,0:T(8,128)} %pad_maximum_fusion), channel_id=1, source_target_pairs={{2,4},{3,5},{10,12},{11,13},{18,20},{19,21},{26,28},{27,29},{34,36... | collective-permute-start | bytes 2359304 | tf_op jit(solution)/shard_map/ppermute | solution.py:289
  116.3 4.8 %copy-start.1 = (bf16[2,1536,256]{2,1,0:T(8,128)(2,1)}, bf16[2,1536,256]{2,1,0:T(8,128)(2,1)S(1)}, u32[]{:S(2)}) copy-start(bf16[2,1536,256]{2,1,0:T(8,128)(2,1)S(1)} %get-tuple-element.19.tables) | copy-start | bytes 4718596
  116.3 2.5 %copy-start.9 = (f32[3,256,1,256]{3,2,1,0:T(1,128)S(1)}, f32[3,256,1,256]{3,2,1,0:T(1,128)}, u32[]{:S(2)}) copy-start(f32[3,256,1,256]{3,2,1,0:T(1,128)} %copy-done.8) | copy-start | bytes 2359300
  118.7 3.0 %collective-permute-start.9 = (f32[3,256,256]{2,1,0:T(8,128)S(1)}, f32[3,256,256]{2,1,0:T(8,128)}, u32[]{:S(2)}, u32[]{:S(2)}) collective-permute-start(f32[3,256,256]{2,1,0:T(8,128)S(1)} %maximum_select_fusion.mine_low), channel_id=1, source_target_pairs={{0,1},{1,0},{2,3},{3,2},{4,5},{5,4},{6,7},{7,6},{8,9},{9,8},{10,11... | collective-permute-start | bytes 2359304 | tf_op jit(solution)/shard_map/ppermute | solution.py:303
  121.1 2.7 %collective-permute-start.11 = (f32[3,256,256]{2,1,0:T(8,128)}, f32[3,256,256]{2,1,0:T(8,128)}, u32[]{:S(2)}, u32[]{:S(2)}) collective-permute-start(f32[3,256,256]{2,1,0:T(8,128)} %select_select_fusion.mine_high), channel_id=1, source_target_pairs={{0,1},{1,0},{2,3},{3,2},{4,5},{5,4},{6,7},{7,6},{8,9},{9,8},{10,11... | collective-permute-start | bytes 2359304 | tf_op jit(solution)/shard_map/ppermute | solution.py:303
  123.9 1.4 copy-start.2
  132.9 1.1 copy-start.4
  134.1 1.2 copy-start.6
  135.2 2.8 %copy-start = (f32[6,256,4,256]{3,2,1,0:T(4,128)S(1)}, f32[6,256,4,256]{3,2,1,0:T(4,128)}, u32[]{:S(2)}) copy-start(f32[6,256,4,256]{3,2,1,0:T(4,128)} %slab.1) | copy-start | bytes 18874372
  138.0 1.4 copy-start.3
  139.4 1.4 copy-start.5
  140.8 1.4 copy-start.7
where the time goes:
time: 155 us; the launch traced here: 153 us
  starting transfers between devices  49.1 us (32%)
  Pallas kernels  42.3 us (27%)
  waiting for transfers between devices  32.4 us (21%)
  local copies, waits for them, and re-layouts  20.8 us (13%)
  other arithmetic  7.62 us (5%)
    pallas_call x1, Pallas kernels, factor_leading(): pl.pallas_call(leading_kernel, out_shape=[jax.ShapeDtypeStruct((2, 6 * NB...  24.4 us
    ppermute x1, waiting for transfers between devices, per_device(): three_low = lax.ppermute(own_low, 'y', [(0, 3)])  13 us
    unnamed x33, local copies, waits for them, and re-layouts  12.4 us
    ppermute x1, waiting for transfers between devices, per_device(): three_high = lax.ppermute(own_high, 'y', [(0, 3)])  11.5 us
    all_to_all x1, starting transfers between devices, per_device(): lax.all_to_all(top.reshape(X * Y * CORE, STEP, NB), PLANE, 0, 0)[:2]  11.2 us
    pallas_call x1, Pallas kernels, update(): pl.pallas_call(update_kernel, grid_spec=pltpu.PrefetchScalarGridSpec(num_...  10.3 us
    all_to_all x1, starting transfers between devices, per_device(): lax.all_to_all(jnp.broadcast_to(pieces, (X * Y * CORE, 3, STEP, NB)), PLA...  8 us
    all_to_all x1, starting transfers between devices, per_device(): lax.all_to_all(tie(raw, pieces, one_high, three_high), ('x', 'z'), 0, 0)  7.96 us
  transfers between devices with their start and end apart: 16, of which 6 were waited for; matrix products, arithmetic and copies ran while one was open for 8% of the time, Pallas kernels for 21%

commit v1 on v0

v1 whole, which is shorter than its diff:
```python
import functools
import jax
import jax.numpy as jnp
from jax import lax
from jax.experimental import pallas as pl
from jax.experimental.pallas import tpu as pltpu
from jax.sharding import Mesh
from jax.sharding import PartitionSpec as P

NB = 256
STEP = 8
HALF = 128
X, Z, Y, CORE = 4, 8, 4, 2
RBL, CBL = 6, 4
PART = RBL // 2
PLANE = ("x", "y", "core")


def times_transposed(left, right):
    return lax.dot_general(
        left, right, (((1,), (1,)), ((), ())), preferred_element_type=jnp.float32
    )


def lane_of(tile, lane):
    return jnp.broadcast_to(tile[:, lane:lane + 1], (STEP, HALF))


def row_of(tile, row):
    return jnp.broadcast_to(tile[row:row + 1, :], tile.shape)


def twice(value):
    return jnp.concatenate([value, value], axis=1)


def symmetric(value):
    rows = lax.broadcasted_iota(jnp.int32, (NB, NB), 0)
    cols = lax.broadcasted_iota(jnp.int32, (NB, NB), 1)
    return jnp.where(rows >= cols, value, value.T)


def factor(work, inverse_ref, upper_ref):
    lanes = lax.broadcasted_iota(jnp.int32, (STEP, NB), 1)
    rows = lax.broadcasted_iota(jnp.int32, (STEP, NB), 0)
    for step in range(NB // STEP):
        j = step * STEP
        half = j // HALF * HALF
        tile = work[j:j + STEP, :]
        diag = tile[:, half:half + HALF]
        cols = [lane_of(diag, j - half + k) for k in range(STEP)]
        left = [[row_of(cols[k], s) if k <= s else None for k in range(STEP)] for s in range(STEP)]
        low = [[None] * STEP for _ in range(STEP)]
        root = [None] * STEP
        inside = (lanes >= j) & (lanes < j + STEP)
        right = [
            jnp.where(inside, jnp.where(lanes == j + i, 1.0, 0.0), row_of(tile, i)) for i in range(STEP)
        ]
        solved = [None] * STEP
        for k in range(STEP):
            root[k] = lax.rsqrt(left[k][k])
            for s in range(k + 1, STEP):
                low[s][k] = left[s][k] * root[k]
            for s in range(k + 1, STEP):
                for m in range(k + 1, s + 1):
                    left[s][m] = left[s][m] - low[s][k] * low[m][k]
            solved[k] = right[k] * twice(root[k])
            for s in range(k + 1, STEP):
                right[s] = right[s] - twice(low[s][k]) * solved[k]
        if step + 1 < NB // STEP:
            rest = work[j + STEP:j + 2 * STEP, :]
            side = rest[:, half:half + HALF]
            ahead = [lane_of(side, j - half + k) for k in range(STEP)]
            total = jnp.where(inside, 0.0, rest)
            for k in range(STEP):
                ahead[k] = ahead[k] * root[k]
                for s in range(k + 1, STEP):
                    ahead[s] = ahead[s] - ahead[k] * low[s][k]
                total = total - twice(ahead[k]) * solved[k]
            work[j + STEP:j + 2 * STEP, :] = total
        weights = [None] * STEP
        for i in range(STEP - 1, -1, -1):
            total = solved[i]
            for s in range(i + 1, STEP):
                total = total - twice(low[s][i]) * weights[s]
            weights[i] = total * twice(root[i])
        for t in range(step + 2, NB // STEP):
            other = work[t * STEP:(t + 1) * STEP, :]
            side = other[:, half:half + HALF]
            total = jnp.where(inside, 0.0, other)
            for i in range(STEP):
                total = total - twice(lane_of(side, j - half + i)) * weights[i]
            work[t * STEP:(t + 1) * STEP, :] = total
        final = solved[0]
        for i in range(1, STEP):
            final = jnp.where(rows == i, solved[i], final)
        block = jnp.zeros((STEP, NB), jnp.float32)
        for i in range(STEP):
            for s in range(i, STEP):
                value = low[s][i] if s > i else left[i][i] * root[i]
                block = jnp.where((rows == i) & (lanes == j + s), twice(value), block)
        inverse_ref[j:j + STEP, :] = jnp.where(lanes < j + STEP, final, 0.0)
        upper_ref[j:j + STEP, :] = jnp.where(lanes >= j + STEP, final, block)


def split(value):
    high = value.astype(jnp.bfloat16)
    rest = value - high.astype(jnp.float32)
    middle = rest.astype(jnp.bfloat16)
    return high, middle, (rest - middle.astype(jnp.float32)).astype(jnp.bfloat16)


def times_table(value, table):
    high, middle, low = split(value)
    wide = jnp.concatenate([high, high, high, middle, middle, low], axis=1)
    return jnp.dot(wide, table, preferred_element_type=jnp.float32)


def leading_kernel(pieces, tables, lower, first_low, source, inverse, upper, work):
    for part in range(2):
        source[part] = pieces[:, 2 * part].reshape(NB, NB)

    @pl.loop(0, 2)
    def _(panel):
        work[...] = symmetric(source[panel])
        factor(work, inverse, upper)
        lower[panel] = upper[...].T
        high, middle, low = split(inverse[...].T)
        for place, term in enumerate([high, middle, low, high, middle, high]):
            tables[panel, place * NB:(place + 1) * NB, :] = term

        @pl.when(panel == 0)
        def _():
            rows = times_table(pieces[:, 1].reshape(NB, NB), tables[0]).astype(jnp.bfloat16)
            first_low[...] = rows.T
            source[1] = source[1] - times_transposed(rows, rows)


def factor_leading(pieces):
    whole = pl.BlockSpec(memory_space=pltpu.VMEM)
    square = pltpu.VMEM((NB, NB), jnp.float32)
    return pl.pallas_call(
        leading_kernel,
        out_shape=[
            jax.ShapeDtypeStruct((2, 6 * NB, NB), jnp.bfloat16),
            pltpu.HBM((2, NB, NB), jnp.float32),
            jax.ShapeDtypeStruct((NB, NB), jnp.bfloat16),
        ],
        in_specs=[whole],
        out_specs=[whole] * 3,
        scratch_shapes=[pltpu.VMEM((2, NB, NB), jnp.float32), square, square, square],
        compiler_params=pltpu.CompilerParams(vmem_limit_bytes=16 * 2**20),
        cost_estimate=pl.CostEstimate(flops=2**10, bytes_accessed=2**10, transcendentals=0),
        name="leading",
    )(pieces)


def panel_rows(raw_first, raw_second, tables, first_low):
    first = times_table(raw_first, tables[0])
    first_bf16 = first.astype(jnp.bfloat16)
    column = raw_second - jnp.dot(first_bf16, first_low[...], preferred_element_type=jnp.float32)
    second = times_table(column, tables[1])
    return first, first_bf16, second


def left_kernel(index, mine, other, tables, lower, first_low, both, keep, give):
    row_block = (index[2] * PART + pl.program_id(0)) * (X * Z) + index[0]
    swap = index[2] == 1
    raw_first = jnp.where(swap, other[0], mine[0])
    raw_second = jnp.where(swap, mine[0], other[0])
    first, first_bf16, second = panel_rows(raw_first, raw_second, tables, first_low)
    first = jnp.where(row_block == 0, lower[0], first)
    second = jnp.where(row_block == 1, lower[1], jnp.where(row_block == 0, 0.0, second))
    both[0, :, :NB] = first.astype(jnp.bfloat16)
    both[0, :, NB:] = second.astype(jnp.bfloat16)
    keep[0] = jnp.where(swap, second, first)
    give[0] = jnp.where(swap, first, second)


def fixed(*shape):
    return pl.BlockSpec(shape, lambda b, _: (0,) * len(shape))


def by_row(*shape):
    return pl.BlockSpec((1,) + shape, lambda b, _: (b,) + (0,) * len(shape))


def left_rows(index, mine, other, tables, lower, first_low):
    panel = pltpu.HBM((PART, NB, NB), jnp.float32)
    return pl.pallas_call(
        left_kernel,
        grid_spec=pltpu.PrefetchScalarGridSpec(
            num_scalar_prefetch=1,
            grid=(PART,),
            in_specs=[by_row(NB, NB)] * 2 + [fixed(2, 6 * NB, NB), fixed(2, NB, NB), fixed(NB, NB)],
            out_specs=[by_row(NB, 2 * NB), by_row(NB, NB), by_row(NB, NB)],
        ),
        out_shape=[pltpu.HBM((PART, NB, 2 * NB), jnp.bfloat16), panel, panel],
        compiler_params=pltpu.CompilerParams(vmem_limit_bytes=20 * 2**20),
        cost_estimate=pl.CostEstimate(flops=2**10, bytes_accessed=2**10, transcendentals=0),
        name="left_rows",
    )(index, mine, other, tables, in_hbm(lower), first_low)


def right_kernel(raw, tables, first_low, out):
    raw_first, raw_second = (raw[:, part].reshape(NB, NB) for part in range(2))
    _, first_bf16, second = panel_rows(raw_first, raw_second, tables, first_low)
    second_bf16 = second.astype(jnp.bfloat16)
    for device in range(X):
        out[device, :, :NB] = first_bf16
        out[device, :, NB:] = second_bf16


def right_rows(raw, tables, first_low):
    whole = pl.BlockSpec(memory_space=pltpu.VMEM)
    return pl.pallas_call(
        right_kernel,
        out_shape=pltpu.HBM((X, NB, 2 * NB), jnp.bfloat16),
        in_specs=[whole] * 3,
        out_specs=whole,
        compiler_params=pltpu.CompilerParams(vmem_limit_bytes=16 * 2**20),
        cost_estimate=pl.CostEstimate(flops=2**10, bytes_accessed=2**10, transcendentals=0),
        name="right_rows",
    )(raw, tables, first_low)


def update_kernel(index, slab, both_mine, both_other, lead_mine, lead_other, right, out):
    col_index = index[1]
    for part in range(2):
        own = index[2] == part
        row_block = (part * PART + pl.program_id(0)) * (X * Z) + index[0]
        both = jnp.where(own, both_mine[0], both_other[0])
        for m in range(CBL):
            change = times_transposed(both, right[m])
            live = (row_block >= 2) & (m * (Y * CORE) + col_index >= 2)
            value = slab[part, 0, :, m, :] - jnp.where(live, change, 0.0)
            if m == 0:
                lead = jnp.where(own, lead_mine[0], lead_other[0])
                value = jnp.where(col_index < 2, lead, value)
            out[part, 0, :, m, :] = value


def update(index, slab, both_mine, both_other, lead_mine, lead_other, right):
    halves = (2, PART) + slab.shape[1:]
    place = pl.BlockSpec((2, 1, NB, CBL, NB), lambda s, _: (0, s, 0, 0, 0))
    return pl.pallas_call(
        update_kernel,
        grid_spec=pltpu.PrefetchScalarGridSpec(
            num_scalar_prefetch=1,
            grid=(PART,),
            in_specs=[
                place, by_row(NB, 2 * NB), by_row(NB, 2 * NB), by_row(NB, NB), by_row(NB, NB),
                fixed(CBL, NB, 2 * NB),
            ],
            out_specs=place,
        ),
        out_shape=jax.ShapeDtypeStruct(halves, jnp.float32),
        compiler_params=pltpu.CompilerParams(vmem_limit_bytes=30 * 2**20),
        cost_estimate=pl.CostEstimate(flops=2**10, bytes_accessed=2**10, transcendentals=0),
        name="update",
    )(
        index, in_hbm(slab.reshape(halves)), in_hbm(both_mine), both_other, in_hbm(lead_mine),
        lead_other, right,
    ).reshape(slab.shape)


def in_hbm(value):
    return pltpu.with_memory_space_constraint(value, pltpu.HBM)


def tie(value, *others):
    return lax.optimization_barrier((value,) + others)[0]


def per_device(slab):
    x, z = lax.axis_index("x"), lax.axis_index("z")
    y, core = lax.axis_index("y"), lax.axis_index("core")
    column = y * CORE + core
    index = jnp.stack([x * Z + z, column, core]).astype(jnp.int32)
    top = slab[0, :, 0, :]
    chunk = NB // Z
    swapped = [(0, 1), (1, 0)]

    def half(which):
        rows = lax.dynamic_slice(slab, (which * PART, 0, 0, 0), (PART, NB, 1, NB))
        return rows.reshape(PART, NB, NB)

    mine_zero = half(core)
    other_zero = lax.ppermute(half(1 - core), "core", swapped)

    def place(k):
        pairs = [(zz * Y * CORE + k, zz * Y * CORE + zz) for zz in range(Z)]
        return lax.ppermute(top, ("z", "y", "core"), pairs)

    scattered = lax.all_to_all(top.reshape(X * Y * CORE, STEP, NB), PLANE, 0, 0)[:2]
    scattered = tie(scattered, mine_zero)
    placed = jnp.stack([place(0), place(1)])
    to_z = jnp.concatenate(
        [
            jnp.broadcast_to(scattered.reshape(1, 2 * STEP, NB), (Z, 2 * STEP, NB)),
            placed.reshape(2, Z, chunk, NB).transpose(1, 0, 2, 3).reshape(Z, 2 * chunk, NB),
        ],
        axis=1,
    )
    mine_one = lax.ppermute(mine_zero, "y", [(0, 1)])
    mine_three = lax.ppermute(mine_zero, "y", [(0, 3)])
    from_z = lax.all_to_all(to_z, "z", 0, 0)
    from_z = tie(from_z, mine_one, mine_three, other_zero)
    pieces = jnp.concatenate([from_z[0, :STEP], from_z[1, :2 * STEP]]).reshape(1, 3, STEP, NB)
    other_one = lax.ppermute(other_zero, "y", [(0, 1)])
    other_three = lax.ppermute(other_zero, "y", [(0, 3)])
    mine_two = lax.ppermute(mine_one, "y", [(1, 2)])
    pieces = lax.all_to_all(
        jnp.broadcast_to(pieces, (X * Y * CORE, 3, STEP, NB)), PLANE, 0, 0
    )
    pieces = tie(pieces, other_one, other_three)
    other_two = lax.ppermute(other_three, "y", [(3, 2)])
    raw = lax.dynamic_index_in_dim(from_z[:, 2 * STEP:], column, 0).reshape(1, 2, chunk, NB)
    raw = jnp.broadcast_to(raw, (Z, 2, chunk, NB))
    raw = lax.all_to_all(tie(raw, pieces, other_one, other_three, mine_two), "z", 0, 0)

    tables, lower, first_low = factor_leading(pieces)

    share = right_rows(raw, tables, first_low)
    right = lax.all_to_all(share, "x", 0, 0)

    def select(zero, one, two, three):
        return jnp.where(y == 0, zero, jnp.where(y == 1, one, jnp.where(y == 3, three, two)))

    mine = select(mine_zero, mine_one, tie(mine_two, share), mine_three)
    other = select(other_zero, other_one, tie(other_two, share), other_three)
    both, keep, give = left_rows(index, mine, other, tables, lower, first_low)
    both_other = lax.ppermute(both, "core", swapped)
    lead_other = lax.ppermute(give, ("y", "core"), swapped)
    return update(index, slab, both, both_other, keep, lead_other, right)


def solution(mesh):
    inner = Mesh(mesh.devices.reshape(X, Z, Y, CORE), ("x", "z", "y", "core"))
    spec = P(None, ("x", "z"), None, ("y", "core"))
    return jax.shard_map(per_device, mesh=inner, in_specs=(spec,), out_specs=spec, check_vma=False)
```

time: 155 us -> 145 us (0.935); the launches traced: 153 us -> 144 us
  local copies, waits for them, and re-layouts: 20.8 us -> 9.77 us
  waiting for transfers between devices: 32.4 us -> 43 us
  other arithmetic: 7.62 us -> 3.05 us
  Pallas kernels: 42.3 us -> 40.5 us
    unnamed x33 -> x9, local copies, waits for them, and re-layouts: 12.4 us -> 2.59 us
    ppermute x10 -> x9, waiting for transfers between devices: 26.7 us -> 35.5 us  [the longest x1 18 us: per_device(): mine_three = lax.ppermute(mine_zero, 'y', [(0, 3)])]
    all_to_all x1 -> x2, waiting for transfers between devices: 0.01 us -> 6.02 us  [the longest x1 6.01 us: per_device(): right = lax.all_to_all(share, 'x', 0, 0)]
    slice x2 -> x0, local copies, waits for them, and re-layouts: 4.39 us -> none  [the longest x1 2.43 us: per_device(): own_high = slab[PART:, :, 0, :]]
    dynamic_slice x0 -> x1, local copies, waits for them, and re-layouts: none -> 3.93 us  [half(): rows = lax.dynamic_slice(slab, (which * PART, 0, 0, 0), (PART, NB, 1, NB))]
    all_to_all x1, starting transfers between devices: 11.2 us -> 7.32 us  [per_device(): lax.all_to_all(top.reshape(X * Y * CORE, STEP, NB), PLANE, 0, 0)[:2]]
    all_to_all x1, starting transfers between devices: 6.83 us -> 10.6 us  [per_device(): from_z = lax.all_to_all(to_z, 'z', 0, 0)]
    all_to_all x1, waiting for transfers between devices: 3.09 us -> 0.01 us  [per_device(): from_z = lax.all_to_all(to_z, 'z', 0, 0)]
  transfers between devices with their start and end apart: 16 -> 16, of which waited for: 6 -> 6; matrix products, arithmetic and copies ran while one was open for 8% -> 6% of each run, Pallas kernels for 21% -> 21%
where the time goes in v1:
time: 145 us; the launch traced here: 144 us
  starting transfers between devices  47.7 us (33%)
  waiting for transfers between devices  43 us (30%)
  Pallas kernels  40.5 us (28%)
  local copies, waits for them, and re-layouts  9.77 us (7%)
  other arithmetic  3.05 us (2%)
    pallas_call x1, Pallas kernels, factor_leading(): pl.pallas_call(leading_kernel, out_shape=[jax.ShapeDtypeStruct((2, 6 * NB...  22.7 us
    ppermute x1, waiting for transfers between devices, per_device(): mine_three = lax.ppermute(mine_zero, 'y', [(0, 3)])  18 us
    ppermute x1, waiting for transfers between devices, per_device(): other_three = lax.ppermute(other_zero, 'y', [(0, 3)])  17.5 us
    all_to_all x1, starting transfers between devices, per_device(): from_z = lax.all_to_all(to_z, 'z', 0, 0)  10.6 us
    pallas_call x1, Pallas kernels, update(): pl.pallas_call(update_kernel, grid_spec=pltpu.PrefetchScalarGridSpec(num_...  9.74 us
    all_to_all x1, starting transfers between devices, per_device(): lax.all_to_all(top.reshape(X * Y * CORE, STEP, NB), PLANE, 0, 0)[:2]  7.32 us
    all_to_all x1, starting transfers between devices, per_device(): lax.all_to_all(tie(raw, pieces, other_one, other_three, mine_two), 'z', 0...  7.21 us
    all_to_all x1, waiting for transfers between devices, per_device(): right = lax.all_to_all(share, 'x', 0, 0)  6.01 us
  transfers between devices with their start and end apart: 16, of which 6 were waited for; matrix products, arithmetic and copies ran while one was open for 6% of the time, Pallas kernels for 21%

profile of v1, /device:TPU:24, one launch (start us, length us, event | category | flops | bytes accessed | tf_op | source)
XLA Modules:
  0.0 144.2 jit_solution(14668679844650908531)
XLA Ops:
  0.0 1.4 slice.15
  1.4 0.7 copy.18
  2.1 0.7 collective-permute-start.3
  2.8 0.7 collective-permute-start.4
  3.5 7.3 %all-to-all-start = ((f32[32,8,256]{2,1,0:T(8,128)}), f32[32,8,256]{2,1,0:T(8,128)S(1)}, u32[]{:S(2)}, u32[]{:S(2)}) async-start(f32[32,8,256]{2,1,0:T(8,128)} %bitcast.34), calls=%async_computation | async-start | bytes 524288 | tf_op jit(solution)/shard_map/all_to_all | solution.py:295
  10.8 3.9 %constant_dynamic-slice_fusion.1 = (f32[3,256,1,256]{3,2,1,0:T(1,128)S(1)}, f32[3,256,1,256]{3,2,1,0:T(1,128)S(1)}) fusion(f32[6,256,4,256]{3,2,1,0:T(4,128)} %param.1, s32[]{:T(128)S(6)} %select_n.46, s32[]{:T(128)S(6)} %select_n.43), kind=kLoop, calls=%fused_computation.12 | loop fusion | bytes 3145736 | tf_op jit(solution)/shard_map/dynamic_slice | solution.py:285
  14.8 0.9 copy-done
  15.6 0.9 copy.17
  16.6 1.3 all-to-all-done
  17.9 0.9 pad_maximum_fusion
  18.8 10.6 %all-to-all-start.1 = ((f32[8,80,256]{2,1,0:T(8,128)}), f32[8,80,256]{2,1,0:T(8,128)S(1)}, u32[]{:S(2)}, u32[]{:S(2)}) async-start(f32[8,80,256]{2,1,0:T(8,128)} %pad_maximum_fusion), calls=%async_computation.1 | async-start | bytes 1310720 | tf_op jit(solution)/shard_map/all_to_all | solution.py:307
  29.5 0.3 collective-permute-start.5
  29.8 0.7 collective-permute-start
  30.5 1.3 collective-permute-start.1
  31.8 1.3 collective-permute-start.7
  33.1 1.6 %collective-permute-start.6 = (f32[3,256,256]{2,1,0:T(8,128)S(1)}, f32[3,256,256]{2,1,0:T(8,128)}, u32[]{:S(2)}, u32[]{:S(2)}) collective-permute-start(f32[3,256,256]{2,1,0:T(8,128)S(1)} %collective-permute-done.5), channel_id=1, source_target_pairs={{0,2},{1,3},{8,10},{9,11},{16,18},{17,19},{24,26},{25,27},{32,34},... | collective-permute-start | bytes 2359304 | tf_op jit(solution)/shard_map/ppermute | solution.py:310
  34.7 1.6 %collective-permute-start.2 = (f32[3,256,256]{2,1,0:T(8,128)S(1)}, f32[3,256,256]{2,1,0:T(8,128)}, u32[]{:S(2)}, u32[]{:S(2)}) collective-permute-start(f32[3,256,256]{2,1,0:T(8,128)S(1)} %collective-permute-done), channel_id=1, source_target_pairs={{2,4},{3,5},{10,12},{11,13},{18,20},{19,21},{26,28},{27,29},{34,36... | collective-permute-start | bytes 2359304 | tf_op jit(solution)/shard_map/ppermute | solution.py:312
  36.3 18.0 %collective-permute-done.1 = f32[3,256,256]{2,1,0:T(8,128)} collective-permute-done((f32[3,256,256]{2,1,0:T(8,128)}, f32[3,256,256]{2,1,0:T(8,128)}, u32[]{:S(2)}, u32[]{:S(2)}) %collective-permute-start.1) | collective-permute-done | bytes 786464 | tf_op jit(solution)/shard_map/ppermute | solution.py:306
  54.3 0.9 broadcast_in_dim.26
  55.2 5.6 %all-to-all-start.2 = ((f32[32,3,8,256]{3,2,1,0:T(8,128)}), f32[32,3,8,256]{3,2,1,0:T(8,128)S(1)}, u32[]{:S(2)}, u32[]{:S(2)}) async-start(f32[32,3,8,256]{3,2,1,0:T(8,128)} %broadcast_in_dim.26), calls=%async_computation.2 | async-start | bytes 1572864 | tf_op jit(solution)/shard_map/all_to_all | solution.py:313
  60.9 17.5 %collective-permute-done.7 = f32[3,256,256]{2,1,0:T(8,128)} collective-permute-done((f32[3,256,256]{2,1,0:T(8,128)S(1)}, f32[3,256,256]{2,1,0:T(8,128)}, u32[]{:S(2)}, u32[]{:S(2)}) %collective-permute-start.7) | collective-permute-done | bytes 786464 | tf_op jit(solution)/shard_map/ppermute | solution.py:311
  78.6 0.8 broadcast_in_dim.24
  79.4 7.2 %all-to-all-start.3 = ((f32[8,2,32,256]{3,2,1,0:T(8,128)}), f32[8,2,32,256]{3,2,1,0:T(8,128)S(1)}, u32[]{:S(2)}, u32[]{:S(2)}) async-start(f32[8,2,32,256]{3,2,1,0:T(8,128)} %broadcast_in_dim.24), calls=%async_computation.3 | async-start | bytes 1048576 | tf_op jit(solution)/shard_map/all_to_all | solution.py:320
  86.6 4.4 %collective-permute-start.8 = (f32[3,256,256]{2,1,0:T(8,128)}, f32[3,256,256]{2,1,0:T(8,128)}, u32[]{:S(2)}, u32[]{:S(2)}) collective-permute-start(f32[3,256,256]{2,1,0:T(8,128)} %collective-permute-done.7), channel_id=1, source_target_pairs={{6,4},{7,5},{14,12},{15,13},{22,20},{23,21},{30,28},{31,29},{38,36... | collective-permute-start | bytes 2359304 | tf_op jit(solution)/shard_map/ppermute | solution.py:317
  91.1 22.7 %leading.1 = (bf16[2,1536,256]{2,1,0:T(8,128)(2,1)S(1)}, f32[2,256,256]{2,1,0:T(8,128)}, bf16[256,256]{1,0:T(8,128)(2,1)S(1)}) custom-call(f32[32,3,8,256]{3,2,1,0:T(8,128)S(1)} %all-to-all-done.2.pieces), custom_call_target="tpu_custom_call" | custom-call | flops 1024 | bytes 1024 | tf_op jit(solution)/shard_map/leading/pallas_call | solution.py:142
  113.8 2.1 %right_rows.1 = bf16[4,256,512]{2,1,0:T(8,128)(2,1)} custom-call(f32[8,2,32,256]{3,2,1,0:T(8,128)S(1)} %all-to-all-done.3.raw, bf16[2,1536,256]{2,1,0:T(8,128)(2,1)S(1)} %get-tuple-element.21.tables, bf16[256,256]{1,0:T(8,128)(2,1)S(1)} %get-tuple-element.22.first_low), custom_call_target="tpu_custom_call" | custom-call | flops 1024 | bytes 1024 | tf_op jit(solution)/shard_map/right_rows/pallas_call | solution.py:216
  115.9 3.7 %all-to-all-start.4 = ((bf16[4,256,512]{2,1,0:T(8,128)(2,1)}), bf16[4,256,512]{2,1,0:T(8,128)(2,1)S(1)}, u32[]{:S(2)}, u32[]{:S(2)}) async-start(bf16[4,256,512]{2,1,0:T(8,128)(2,1)} %right_rows.1), calls=%async_computation.4 | async-start | bytes 2097152 | tf_op jit(solution)/shard_map/all_to_all | solution.py:325
  119.6 2.0 %select_select_fusion = (f32[3,256,256]{2,1,0:T(8,128)S(1)}, f32[3,256,256]{2,1,0:T(8,128)S(1)}) fusion(f32[3,256,256]{2,1,0:T(8,128)} %copy-done.1, f32[3,256,256]{2,1,0:T(8,128)} %collective-permute-done.6, f32[3,256,256]{2,1,0:T(8,128)} %collective-permute-done.7, f32[3,256,256]{2,1,0:T(8,128)} %collective-permute-done.8, pred[]{:T(512)S(6)} %eq.14, ...), kind=kLoop, calls=%fused_computation.2 | loop fusion | flops 1179648 | bytes 7864323 | tf_op jit(solution)/shard_map/jit(_where)/select_n | solution.py:328
  121.7 6.0 %left_rows.1 = (bf16[3,256,512]{2,1,0:T(8,128)(2,1)}, f32[3,256,256]{2,1,0:T(8,128)}, f32[3,256,256]{2,1,0:T(8,128)}) custom-call(s32[3]{0:T(128)S(1)} %pad_add_fusion.index, f32[3,256,256]{2,1,0:T(8,128)S(1)} %get-tuple-element.34.mine, f32[3,256,256]{2,1,0:T(8,128)S(1)} %get-tuple-element.33.other, bf16[2,1536,256]{2,1,0:T(8,128)(2,1)S(1)} %get-tuple-element.21.tables, ...), custom_call_target="tpu_custom_call" | custom-call | flops 1024 | bytes 1024 | tf_op jit(solution)/shard_map/left_rows/pallas_call | solution.py:190
  127.6 0.7 collective-permute-start.10
  128.4 6.0 %all-to-all-done.4.right = bf16[4,256,512]{2,1,0:T(8,128)(2,1)S(1)} async-done(((bf16[4,256,512]{2,1,0:T(8,128)(2,1)}), bf16[4,256,512]{2,1,0:T(8,128)(2,1)S(1)}, u32[]{:S(2)}, u32[]{:S(2)}) %all-to-all-start.4) | async-done | bytes 1048608 | tf_op jit(solution)/shard_map/all_to_all | solution.py:325
  134.4 9.7 %update.1 = f32[2,3,256,4,256]{4,3,2,1,0:T(4,128)} custom-call(s32[3]{0:T(128)S(1)} %pad_add_fusion.index, f32[2,3,256,4,256]{4,3,2,1,0:T(4,128)} %bitcast.35, bf16[3,256,512]{2,1,0:T(8,128)(2,1)} %get-tuple-element.26.both_mine, bf16[3,256,512]{2,1,0:T(8,128)(2,1)S(1)} %collective-permute-done.9.both_other, f32[3,256,256]{2,1,0:T(8,128)} %get-tuple-element.27.lead_mine, ...), custom_call_target="tpu_custom_call" | custom-call | flops 1024 | bytes 1024 | tf_op jit(solution)/shard_map/update/pallas_call | solution.py:246
  (28 shorter events, 0.6 us)
Async XLA Ops:
  2.1 15.7 %collective-permute-start.3 = (f32[256,256]{1,0:T(8,128)}, f32[256,256]{1,0:T(8,128)S(1)}, u32[]{:S(2)}, u32[]{:S(2)}) collective-permute-start(f32[256,256]{1,0:T(8,128)} %bitcast.25.clone.2), channel_id=1, source_target_pairs={{0,0},{8,9},{16,18},{24,27},{32,36},{40,45},{48,54},{56,63},{64,64... | collective-permute-start | bytes 786440 | tf_op jit(solution)/shard_map/ppermute | solution.py:293
  2.8 15.0 %collective-permute-start.4 = (f32[256,256]{1,0:T(8,128)}, f32[256,256]{1,0:T(8,128)S(1)}, u32[]{:S(2)}, u32[]{:S(2)}) collective-permute-start(f32[256,256]{1,0:T(8,128)} %bitcast.25.clone.2), channel_id=1, source_target_pairs={{1,0},{9,9},{17,18},{25,27},{33,36},{41,45},{49,54},{57,63},{65,64... | collective-permute-start | bytes 786440 | tf_op jit(solution)/shard_map/ppermute | solution.py:293
  3.5 14.3 %all-to-all-start = ((f32[32,8,256]{2,1,0:T(8,128)}), f32[32,8,256]{2,1,0:T(8,128)S(1)}, u32[]{:S(2)}, u32[]{:S(2)}) async-start(f32[32,8,256]{2,1,0:T(8,128)} %bitcast.34), calls=%async_computation | async-start | bytes 524288 | tf_op jit(solution)/shard_map/all_to_all | solution.py:295
  14.8 0.9 copy-start
  18.8 35.5 %all-to-all-start.1 = ((f32[8,80,256]{2,1,0:T(8,128)}), f32[8,80,256]{2,1,0:T(8,128)S(1)}, u32[]{:S(2)}, u32[]{:S(2)}) async-start(f32[8,80,256]{2,1,0:T(8,128)} %pad_maximum_fusion), calls=%async_computation.1 | async-start | bytes 1310720 | tf_op jit(solution)/shard_map/all_to_all | solution.py:307
  29.5 2.4 %collective-permute-start.5 = (f32[3,256,256]{2,1,0:T(8,128)S(1)}, f32[3,256,256]{2,1,0:T(8,128)S(1)}, u32[]{:S(2)}, u32[]{:S(2)}) collective-permute-start(f32[3,256,256]{2,1,0:T(8,128)S(1)} %bitcast.39), channel_id=1, source_target_pairs={{0,1},{1,0},{2,3},{3,2},{4,5},{5,4},{6,7},{7,6},{8,9},{9,8},{10,11... | collective-permute-start | bytes 2359304 | tf_op jit(solution)/shard_map/ppermute | solution.py:289
  29.8 4.9 %collective-permute-start = (f32[3,256,256]{2,1,0:T(8,128)}, f32[3,256,256]{2,1,0:T(8,128)S(1)}, u32[]{:S(2)}, u32[]{:S(2)}) collective-permute-start(f32[3,256,256]{2,1,0:T(8,128)} %bitcast.37), channel_id=1, source_target_pairs={{0,2},{1,3},{8,10},{9,11},{16,18},{17,19},{24,26},{25,27},{32,34},... | collective-permute-start | bytes 2359304 | tf_op jit(solution)/shard_map/ppermute | solution.py:305
  30.5 23.8 %collective-permute-start.1 = (f32[3,256,256]{2,1,0:T(8,128)}, f32[3,256,256]{2,1,0:T(8,128)}, u32[]{:S(2)}, u32[]{:S(2)}) collective-permute-start(f32[3,256,256]{2,1,0:T(8,128)} %bitcast.38), channel_id=1, source_target_pairs={{0,6},{1,7},{8,14},{9,15},{16,22},{17,23},{24,30},{25,31},{32,38},... | collective-permute-start | bytes 2359304 | tf_op jit(solution)/shard_map/ppermute | solution.py:306
  31.8 59.2 %copy-start.1 = (f32[3,256,256]{2,1,0:T(8,128)}, f32[3,256,256]{2,1,0:T(8,128)S(1)}, u32[]{:S(2)}) copy-start(f32[3,256,256]{2,1,0:T(8,128)S(1)} %collective-permute-done.5) | copy-start | bytes 2359300
  31.8 46.5 %collective-permute-start.7 = (f32[3,256,256]{2,1,0:T(8,128)S(1)}, f32[3,256,256]{2,1,0:T(8,128)}, u32[]{:S(2)}, u32[]{:S(2)}) collective-permute-start(f32[3,256,256]{2,1,0:T(8,128)S(1)} %collective-permute-done.5), channel_id=1, source_target_pairs={{0,6},{1,7},{8,14},{9,15},{16,22},{17,23},{24,30},{25,31},{32,38},... | collective-permute-start | bytes 2359304 | tf_op jit(solution)/shard_map/ppermute | solution.py:311
  33.1 45.3 %collective-permute-start.6 = (f32[3,256,256]{2,1,0:T(8,128)S(1)}, f32[3,256,256]{2,1,0:T(8,128)}, u32[]{:S(2)}, u32[]{:S(2)}) collective-permute-start(f32[3,256,256]{2,1,0:T(8,128)S(1)} %collective-permute-done.5), channel_id=1, source_target_pairs={{0,2},{1,3},{8,10},{9,11},{16,18},{17,19},{24,26},{25,27},{32,34},... | collective-permute-start | bytes 2359304 | tf_op jit(solution)/shard_map/ppermute | solution.py:310
  34.7 56.3 %copy-start.2 = (f32[3,256,256]{2,1,0:T(8,128)}, f32[3,256,256]{2,1,0:T(8,128)S(1)}, u32[]{:S(2)}) copy-start(f32[3,256,256]{2,1,0:T(8,128)S(1)} %collective-permute-done) | copy-start | bytes 2359300
  34.7 43.9 %collective-permute-start.2 = (f32[3,256,256]{2,1,0:T(8,128)S(1)}, f32[3,256,256]{2,1,0:T(8,128)}, u32[]{:S(2)}, u32[]{:S(2)}) collective-permute-start(f32[3,256,256]{2,1,0:T(8,128)S(1)} %collective-permute-done), channel_id=1, source_target_pairs={{2,4},{3,5},{10,12},{11,13},{18,20},{19,21},{26,28},{27,29},{34,36... | collective-permute-start | bytes 2359304 | tf_op jit(solution)/shard_map/ppermute | solution.py:312
  55.2 23.3 %all-to-all-start.2 = ((f32[32,3,8,256]{3,2,1,0:T(8,128)}), f32[32,3,8,256]{3,2,1,0:T(8,128)S(1)}, u32[]{:S(2)}, u32[]{:S(2)}) async-start(f32[32,3,8,256]{3,2,1,0:T(8,128)} %broadcast_in_dim.26), calls=%async_computation.2 | async-start | bytes 1572864 | tf_op jit(solution)/shard_map/all_to_all | solution.py:313
  79.4 34.4 %all-to-all-start.3 = ((f32[8,2,32,256]{3,2,1,0:T(8,128)}), f32[8,2,32,256]{3,2,1,0:T(8,128)S(1)}, u32[]{:S(2)}, u32[]{:S(2)}) async-start(f32[8,2,32,256]{3,2,1,0:T(8,128)} %broadcast_in_dim.24), calls=%async_computation.3 | async-start | bytes 1048576 | tf_op jit(solution)/shard_map/all_to_all | solution.py:320
  86.6 33.0 %collective-permute-start.8 = (f32[3,256,256]{2,1,0:T(8,128)}, f32[3,256,256]{2,1,0:T(8,128)}, u32[]{:S(2)}, u32[]{:S(2)}) collective-permute-start(f32[3,256,256]{2,1,0:T(8,128)} %collective-permute-done.7), channel_id=1, source_target_pairs={{6,4},{7,5},{14,12},{15,13},{22,20},{23,21},{30,28},{31,29},{38,36... | collective-permute-start | bytes 2359304 | tf_op jit(solution)/shard_map/ppermute | solution.py:317
  115.9 18.6 %all-to-all-start.4 = ((bf16[4,256,512]{2,1,0:T(8,128)(2,1)}), bf16[4,256,512]{2,1,0:T(8,128)(2,1)S(1)}, u32[]{:S(2)}, u32[]{:S(2)}) async-start(bf16[4,256,512]{2,1,0:T(8,128)(2,1)} %right_rows.1), calls=%async_computation.4 | async-start | bytes 2097152 | tf_op jit(solution)/shard_map/all_to_all | solution.py:325
  127.6 6.8 %collective-permute-start.10 = (f32[3,256,256]{2,1,0:T(8,128)}, f32[3,256,256]{2,1,0:T(8,128)S(1)}, u32[]{:S(2)}, u32[]{:S(2)}) collective-permute-start(f32[3,256,256]{2,1,0:T(8,128)} %get-tuple-element.28), channel_id=1, source_target_pairs={{0,1},{1,0},{8,9},{9,8},{16,17},{17,16},{24,25},{25,24},{32,33},{3... | collective-permute-start | bytes 2359304 | tf_op jit(solution)/shard_map/ppermute | solution.py:334
  128.3 6.1 %collective-permute-start.9 = (bf16[3,256,512]{2,1,0:T(8,128)(2,1)}, bf16[3,256,512]{2,1,0:T(8,128)(2,1)S(1)}, u32[]{:S(2)}, u32[]{:S(2)}) collective-permute-start(bf16[3,256,512]{2,1,0:T(8,128)(2,1)} %get-tuple-element.26.both_mine), channel_id=1, source_target_pairs={{0,1},{1,0},{2,3},{3,2},{4,5},{5,4},{6,7},{7,6},{8,9},{9,8},{10,11... | collective-permute-start | bytes 2359304 | tf_op jit(solution)/shard_map/ppermute | solution.py:333

commit v2 on v1

--- a/solution.py
+++ b/solution.py
@@ -30,25 +30,19 @@
     return jnp.broadcast_to(tile[row:row + 1, :], tile.shape)
 
 
-def twice(value):
-    return jnp.concatenate([value, value], axis=1)
-
-
 def symmetric(value):
-    rows = lax.broadcasted_iota(jnp.int32, (NB, NB), 0)
-    cols = lax.broadcasted_iota(jnp.int32, (NB, NB), 1)
+    rows = lax.broadcasted_iota(jnp.int32, value.shape, 0)
+    cols = lax.broadcasted_iota(jnp.int32, value.shape, 1)
     return jnp.where(rows >= cols, value, value.T)
 
 
 def factor(work, inverse_ref, upper_ref):
-    lanes = lax.broadcasted_iota(jnp.int32, (STEP, NB), 1)
-    rows = lax.broadcasted_iota(jnp.int32, (STEP, NB), 0)
-    for step in range(NB // STEP):
+    lanes = lax.broadcasted_iota(jnp.int32, (STEP, HALF), 1)
+    rows = lax.broadcasted_iota(jnp.int32, (STEP, HALF), 0)
+    for step in range(HALF // STEP):
         j = step * STEP
-        half = j // HALF * HALF
         tile = work[j:j + STEP, :]
-        diag = tile[:, half:half + HALF]
-        cols = [lane_of(diag, j - half + k) for k in range(STEP)]
+        cols = [lane_of(tile, j + k) for k in range(STEP)]
         left = [[row_of(cols[k], s) if k <= s else None for k in range(STEP)] for s in range(STEP)]
         low = [[None] * STEP for _ in range(STEP)]
         root = [None] * STEP
@@ -64,41 +58,39 @@
             for s in range(k + 1, STEP):
                 for m in range(k + 1, s + 1):
                     left[s][m] = left[s][m] - low[s][k] * low[m][k]
-            solved[k] = right[k] * twice(root[k])
+            solved[k] = right[k] * root[k]
             for s in range(k + 1, STEP):
-                right[s] = right[s] - twice(low[s][k]) * solved[k]
-        if step + 1 < NB // STEP:
+                right[s] = right[s] - low[s][k] * solved[k]
+        if step + 1 < HALF // STEP:
             rest = work[j + STEP:j + 2 * STEP, :]
-            side = rest[:, half:half + HALF]
-            ahead = [lane_of(side, j - half + k) for k in range(STEP)]
+            ahead = [lane_of(rest, j + k) for k in range(STEP)]
             total = jnp.where(inside, 0.0, rest)
             for k in range(STEP):
                 ahead[k] = ahead[k] * root[k]
                 for s in range(k + 1, STEP):
                     ahead[s] = ahead[s] - ahead[k] * low[s][k]
-                total = total - twice(ahead[k]) * solved[k]
+                total = total - ahead[k] * solved[k]
             work[j + STEP:j + 2 * STEP, :] = total
         weights = [None] * STEP
         for i in range(STEP - 1, -1, -1):
             total = solved[i]
             for s in range(i + 1, STEP):
-                total = total - twice(low[s][i]) * weights[s]
-            weights[i] = total * twice(root[i])
-        for t in range(step + 2, NB // STEP):
+                total = total - low[s][i] * weights[s]
+            weights[i] = total * root[i]
+        for t in range(step + 2, HALF // STEP):
             other = work[t * STEP:(t + 1) * STEP, :]
-            side = other[:, half:half + HALF]
             total = jnp.where(inside, 0.0, other)
             for i in range(STEP):
-                total = total - twice(lane_of(side, j - half + i)) * weights[i]
+                total = total - lane_of(other, j + i) * weights[i]
             work[t * STEP:(t + 1) * STEP, :] = total
         final = solved[0]
         for i in range(1, STEP):
             final = jnp.where(rows == i, solved[i], final)
-        block = jnp.zeros((STEP, NB), jnp.float32)
+        block = jnp.zeros((STEP, HALF), jnp.float32)
         for i in range(STEP):
             for s in range(i, STEP):
                 value = low[s][i] if s > i else left[i][i] * root[i]
-                block = jnp.where((rows == i) & (lanes == j + s), twice(value), block)
+                block = jnp.where((rows == i) & (lanes == j + s), value, block)
         inverse_ref[j:j + STEP, :] = jnp.where(lanes < j + STEP, final, 0.0)
         upper_ref[j:j + STEP, :] = jnp.where(lanes >= j + STEP, final, block)
 
@@ -116,29 +108,52 @@
     return jnp.dot(wide, table, preferred_element_type=jnp.float32)
 
 
-def leading_kernel(pieces, tables, lower, first_low, source, inverse, upper, work):
+def table_of(value):
+    high, middle, low = split(value)
+    return jnp.concatenate([high, middle, low, high, middle, high])
+
+
+def leading_kernel(pieces, tables, lower, first_low, source, first_inverse, below, inverse, upper, work):
     for part in range(2):
         source[part] = pieces[:, 2 * part].reshape(NB, NB)
-
-    @pl.loop(0, 2)
-    def _(panel):
-        work[...] = symmetric(source[panel])
+    work[...] = symmetric(source[0, :HALF, :HALF])
+    zeros = jnp.zeros((HALF, HALF), jnp.float32)
+
+    @pl.loop(0, 4)
+    def _(part):
+        panel = part // 2
         factor(work, inverse, upper)
-        lower[panel] = upper[...].T
-        high, middle, low = split(inverse[...].T)
-        for place, term in enumerate([high, middle, low, high, middle, high]):
-            tables[panel, place * NB:(place + 1) * NB, :] = term
-
-        @pl.when(panel == 0)
+
+        @pl.when(part % 2 == 0)
+        def _():
+            first_inverse[...] = inverse[...]
+            side = times_table(source[panel, HALF:, :HALF], table_of(inverse[...].T))
+            below[...] = side
+            work[...] = symmetric(source[panel, HALF:, HALF:] - times_table(side, table_of(side.T)))
+            lower[panel, :HALF, :HALF] = upper[...].T
+            lower[panel, :HALF, HALF:] = zeros
+            lower[panel, HALF:, :HALF] = side
+
+        @pl.when(part % 2 == 1)
+        def _():
+            corner = times_table(below[...], table_of(first_inverse[...]))
+            corner = -times_table(inverse[...], table_of(corner))
+            top = jnp.concatenate([first_inverse[...].T, corner.T], axis=1)
+            bottom = jnp.concatenate([zeros, inverse[...].T], axis=1)
+            tables[panel] = table_of(jnp.concatenate([top, bottom]))
+            lower[panel, HALF:, HALF:] = upper[...].T
+
+        @pl.when(part == 1)
         def _():
             rows = times_table(pieces[:, 1].reshape(NB, NB), tables[0]).astype(jnp.bfloat16)
             first_low[...] = rows.T
             source[1] = source[1] - times_transposed(rows, rows)
+            work[...] = symmetric(source[1, :HALF, :HALF])
 
 
 def factor_leading(pieces):
     whole = pl.BlockSpec(memory_space=pltpu.VMEM)
-    square = pltpu.VMEM((NB, NB), jnp.float32)
+    square = pltpu.VMEM((HALF, HALF), jnp.float32)
     return pl.pallas_call(
         leading_kernel,
         out_shape=[
@@ -148,7 +163,7 @@
         ],
         in_specs=[whole],
         out_specs=[whole] * 3,
-        scratch_shapes=[pltpu.VMEM((2, NB, NB), jnp.float32), square, square, square],
+        scratch_shapes=[pltpu.VMEM((2, NB, NB), jnp.float32)] + [square] * 5,
         compiler_params=pltpu.CompilerParams(vmem_limit_bytes=16 * 2**20),
         cost_estimate=pl.CostEstimate(flops=2**10, bytes_accessed=2**10, transcendentals=0),
         name="leading",

time: 145 us -> 142 us (0.979)
  Pallas kernels: 40.5 us -> 37.2 us
    pallas_call x1, Pallas kernels: 22.7 us -> 19.4 us  [factor_leading(): pl.pallas_call(leading_kernel, out_shape=[jax.ShapeDtypeStruct((2, 6 * NB...]
  transfers between devices with their start and end apart: 16 -> 16, of which waited for: 6 -> 6; matrix products, arithmetic and copies ran while one was open for 6% -> 6% of each run, Pallas kernels for 21% -> 19%
where the time goes in v2:
time: 142 us; the launch traced here: 141 us
  starting transfers between devices  47.5 us (33%)
  waiting for transfers between devices  43.2 us (30%)
  Pallas kernels  37.2 us (26%)
  local copies, waits for them, and re-layouts  9.77 us (7%)
  other arithmetic  3.05 us (2%)
    pallas_call x1, Pallas kernels, factor_leading(): pl.pallas_call(leading_kernel, out_shape=[jax.ShapeDtypeStruct((2, 6 * NB...  19.4 us
    ppermute x1, waiting for transfers between devices, per_device(): mine_three = lax.ppermute(mine_zero, 'y', [(0, 3)])  18 us
    ppermute x1, waiting for transfers between devices, per_device(): other_three = lax.ppermute(other_zero, 'y', [(0, 3)])  17.5 us
    all_to_all x1, starting transfers between devices, per_device(): from_z = lax.all_to_all(to_z, 'z', 0, 0)  10.6 us
    pallas_call x1, Pallas kernels, update(): pl.pallas_call(update_kernel, grid_spec=pltpu.PrefetchScalarGridSpec(num_...  9.75 us
    all_to_all x1, starting transfers between devices, per_device(): lax.all_to_all(top.reshape(X * Y * CORE, STEP, NB), PLANE, 0, 0)[:2]  7.32 us
    all_to_all x1, starting transfers between devices, per_device(): lax.all_to_all(tie(raw, pieces, other_one, other_three, mine_two), 'z', 0...  7.21 us
    all_to_all x1, waiting for transfers between devices, per_device(): right = lax.all_to_all(share, 'x', 0, 0)  6.23 us
  transfers between devices with their start and end apart: 16, of which 6 were waited for; matrix products, arithmetic and copies ran while one was open for 6% of the time, Pallas kernels for 19%

profile of v2, /device:TPU:24, one launch (start us, length us, event | category | flops | bytes accessed | tf_op | source)
XLA Modules:
  0.0 140.9 jit_solution(5104029664947578582)
XLA Ops:
  0.0 1.4 slice.15
  1.4 0.7 copy.18
  2.1 0.7 collective-permute-start.3
  2.8 0.7 collective-permute-start.4
  3.5 7.3 %all-to-all-start = ((f32[32,8,256]{2,1,0:T(8,128)}), f32[32,8,256]{2,1,0:T(8,128)S(1)}, u32[]{:S(2)}, u32[]{:S(2)}) async-start(f32[32,8,256]{2,1,0:T(8,128)} %bitcast.34), calls=%async_computation | async-start | bytes 524288 | tf_op jit(solution)/shard_map/all_to_all | solution.py:310
  10.8 3.9 %constant_dynamic-slice_fusion.1 = (f32[3,256,1,256]{3,2,1,0:T(1,128)S(1)}, f32[3,256,1,256]{3,2,1,0:T(1,128)S(1)}) fusion(f32[6,256,4,256]{3,2,1,0:T(4,128)} %param.1, s32[]{:T(128)S(6)} %select_n.46, s32[]{:T(128)S(6)} %select_n.43), kind=kLoop, calls=%fused_computation.12 | loop fusion | bytes 3145736 | tf_op jit(solution)/shard_map/dynamic_slice | solution.py:300
  14.8 0.9 copy-done
  15.6 0.9 copy.17
  16.6 1.3 all-to-all-done
  17.9 0.9 pad_maximum_fusion
  18.8 10.6 %all-to-all-start.1 = ((f32[8,80,256]{2,1,0:T(8,128)}), f32[8,80,256]{2,1,0:T(8,128)S(1)}, u32[]{:S(2)}, u32[]{:S(2)}) async-start(f32[8,80,256]{2,1,0:T(8,128)} %pad_maximum_fusion), calls=%async_computation.1 | async-start | bytes 1310720 | tf_op jit(solution)/shard_map/all_to_all | solution.py:322
  29.5 0.3 collective-permute-start.5
  29.8 0.7 collective-permute-start
  30.5 1.3 collective-permute-start.1
  31.8 1.3 collective-permute-start.7
  33.1 1.6 %collective-permute-start.6 = (f32[3,256,256]{2,1,0:T(8,128)S(1)}, f32[3,256,256]{2,1,0:T(8,128)}, u32[]{:S(2)}, u32[]{:S(2)}) collective-permute-start(f32[3,256,256]{2,1,0:T(8,128)S(1)} %collective-permute-done.5), channel_id=1, source_target_pairs={{0,2},{1,3},{8,10},{9,11},{16,18},{17,19},{24,26},{25,27},{32,34},... | collective-permute-start | bytes 2359304 | tf_op jit(solution)/shard_map/ppermute | solution.py:325
  34.7 1.6 %collective-permute-start.2 = (f32[3,256,256]{2,1,0:T(8,128)S(1)}, f32[3,256,256]{2,1,0:T(8,128)}, u32[]{:S(2)}, u32[]{:S(2)}) collective-permute-start(f32[3,256,256]{2,1,0:T(8,128)S(1)} %collective-permute-done), channel_id=1, source_target_pairs={{2,4},{3,5},{10,12},{11,13},{18,20},{19,21},{26,28},{27,29},{34,36... | collective-permute-start | bytes 2359304 | tf_op jit(solution)/shard_map/ppermute | solution.py:327
  36.3 18.0 %collective-permute-done.1 = f32[3,256,256]{2,1,0:T(8,128)} collective-permute-done((f32[3,256,256]{2,1,0:T(8,128)}, f32[3,256,256]{2,1,0:T(8,128)}, u32[]{:S(2)}, u32[]{:S(2)}) %collective-permute-start.1) | collective-permute-done | bytes 786464 | tf_op jit(solution)/shard_map/ppermute | solution.py:321
  54.3 0.9 broadcast_in_dim.26
  55.2 5.6 %all-to-all-start.2 = ((f32[32,3,8,256]{3,2,1,0:T(8,128)}), f32[32,3,8,256]{3,2,1,0:T(8,128)S(1)}, u32[]{:S(2)}, u32[]{:S(2)}) async-start(f32[32,3,8,256]{3,2,1,0:T(8,128)} %broadcast_in_dim.26), calls=%async_computation.2 | async-start | bytes 1572864 | tf_op jit(solution)/shard_map/all_to_all | solution.py:328
  60.9 17.5 %collective-permute-done.7 = f32[3,256,256]{2,1,0:T(8,128)} collective-permute-done((f32[3,256,256]{2,1,0:T(8,128)S(1)}, f32[3,256,256]{2,1,0:T(8,128)}, u32[]{:S(2)}, u32[]{:S(2)}) %collective-permute-start.7) | collective-permute-done | bytes 786464 | tf_op jit(solution)/shard_map/ppermute | solution.py:326
  78.6 0.8 broadcast_in_dim.24
  79.4 7.2 %all-to-all-start.3 = ((f32[8,2,32,256]{3,2,1,0:T(8,128)}), f32[8,2,32,256]{3,2,1,0:T(8,128)S(1)}, u32[]{:S(2)}, u32[]{:S(2)}) async-start(f32[8,2,32,256]{3,2,1,0:T(8,128)} %broadcast_in_dim.24), calls=%async_computation.3 | async-start | bytes 1048576 | tf_op jit(solution)/shard_map/all_to_all | solution.py:335
  86.6 4.4 %collective-permute-start.8 = (f32[3,256,256]{2,1,0:T(8,128)}, f32[3,256,256]{2,1,0:T(8,128)}, u32[]{:S(2)}, u32[]{:S(2)}) collective-permute-start(f32[3,256,256]{2,1,0:T(8,128)} %collective-permute-done.7), channel_id=1, source_target_pairs={{6,4},{7,5},{14,12},{15,13},{22,20},{23,21},{30,28},{31,29},{38,36... | collective-permute-start | bytes 2359304 | tf_op jit(solution)/shard_map/ppermute | solution.py:332
  91.1 19.4 %leading.1 = (bf16[2,1536,256]{2,1,0:T(8,128)(2,1)S(1)}, f32[2,256,256]{2,1,0:T(8,128)}, bf16[256,256]{1,0:T(8,128)(2,1)S(1)}) custom-call(f32[32,3,8,256]{3,2,1,0:T(8,128)S(1)} %all-to-all-done.2.pieces), custom_call_target="tpu_custom_call" | custom-call | flops 1024 | bytes 1024 | tf_op jit(solution)/shard_map/leading/pallas_call | solution.py:157
  110.5 2.1 %right_rows.1 = bf16[4,256,512]{2,1,0:T(8,128)(2,1)} custom-call(f32[8,2,32,256]{3,2,1,0:T(8,128)S(1)} %all-to-all-done.3.raw, bf16[2,1536,256]{2,1,0:T(8,128)(2,1)S(1)} %get-tuple-element.21.tables, bf16[256,256]{1,0:T(8,128)(2,1)S(1)} %get-tuple-element.22.first_low), custom_call_target="tpu_custom_call" | custom-call | flops 1024 | bytes 1024 | tf_op jit(solution)/shard_map/right_rows/pallas_call | solution.py:231
  112.6 3.5 %all-to-all-start.4 = ((bf16[4,256,512]{2,1,0:T(8,128)(2,1)}), bf16[4,256,512]{2,1,0:T(8,128)(2,1)S(1)}, u32[]{:S(2)}, u32[]{:S(2)}) async-start(bf16[4,256,512]{2,1,0:T(8,128)(2,1)} %right_rows.1), calls=%async_computation.4 | async-start | bytes 2097152 | tf_op jit(solution)/shard_map/all_to_all | solution.py:340
  116.1 2.0 %select_select_fusion = (f32[3,256,256]{2,1,0:T(8,128)S(1)}, f32[3,256,256]{2,1,0:T(8,128)S(1)}) fusion(f32[3,256,256]{2,1,0:T(8,128)} %copy-done.1, f32[3,256,256]{2,1,0:T(8,128)} %collective-permute-done.6, f32[3,256,256]{2,1,0:T(8,128)} %collective-permute-done.7, f32[3,256,256]{2,1,0:T(8,128)} %collective-permute-done.8, pred[]{:T(512)S(6)} %eq.14, ...), kind=kLoop, calls=%fused_computation.2 | loop fusion | flops 1179648 | bytes 7864323 | tf_op jit(solution)/shard_map/jit(_where)/select_n | solution.py:343
  118.1 6.0 %left_rows.1 = (bf16[3,256,512]{2,1,0:T(8,128)(2,1)}, f32[3,256,256]{2,1,0:T(8,128)}, f32[3,256,256]{2,1,0:T(8,128)}) custom-call(s32[3]{0:T(128)S(1)} %pad_add_fusion.index, f32[3,256,256]{2,1,0:T(8,128)S(1)} %get-tuple-element.34.mine, f32[3,256,256]{2,1,0:T(8,128)S(1)} %get-tuple-element.33.other, bf16[2,1536,256]{2,1,0:T(8,128)(2,1)S(1)} %get-tuple-element.21.tables, ...), custom_call_target="tpu_custom_call" | custom-call | flops 1024 | bytes 1024 | tf_op jit(solution)/shard_map/left_rows/pallas_call | solution.py:205
  124.1 0.7 collective-permute-start.10
  124.9 6.2 %all-to-all-done.4.right = bf16[4,256,512]{2,1,0:T(8,128)(2,1)S(1)} async-done(((bf16[4,256,512]{2,1,0:T(8,128)(2,1)}), bf16[4,256,512]{2,1,0:T(8,128)(2,1)S(1)}, u32[]{:S(2)}, u32[]{:S(2)}) %all-to-all-start.4) | async-done | bytes 1048608 | tf_op jit(solution)/shard_map/all_to_all | solution.py:340
  131.1 9.7 %update.1 = f32[2,3,256,4,256]{4,3,2,1,0:T(4,128)} custom-call(s32[3]{0:T(128)S(1)} %pad_add_fusion.index, f32[2,3,256,4,256]{4,3,2,1,0:T(4,128)} %bitcast.35, bf16[3,256,512]{2,1,0:T(8,128)(2,1)} %get-tuple-element.26.both_mine, bf16[3,256,512]{2,1,0:T(8,128)(2,1)S(1)} %collective-permute-done.9.both_other, f32[3,256,256]{2,1,0:T(8,128)} %get-tuple-element.27.lead_mine, ...), custom_call_target="tpu_custom_call" | custom-call | flops 1024 | bytes 1024 | tf_op jit(solution)/shard_map/update/pallas_call | solution.py:261
  (28 shorter events, 0.6 us)
Async XLA Ops:
  2.1 15.7 %collective-permute-start.3 = (f32[256,256]{1,0:T(8,128)}, f32[256,256]{1,0:T(8,128)S(1)}, u32[]{:S(2)}, u32[]{:S(2)}) collective-permute-start(f32[256,256]{1,0:T(8,128)} %bitcast.25.clone.2), channel_id=1, source_target_pairs={{0,0},{8,9},{16,18},{24,27},{32,36},{40,45},{48,54},{56,63},{64,64... | collective-permute-start | bytes 786440 | tf_op jit(solution)/shard_map/ppermute | solution.py:308
  2.8 15.0 %collective-permute-start.4 = (f32[256,256]{1,0:T(8,128)}, f32[256,256]{1,0:T(8,128)S(1)}, u32[]{:S(2)}, u32[]{:S(2)}) collective-permute-start(f32[256,256]{1,0:T(8,128)} %bitcast.25.clone.2), channel_id=1, source_target_pairs={{1,0},{9,9},{17,18},{25,27},{33,36},{41,45},{49,54},{57,63},{65,64... | collective-permute-start | bytes 786440 | tf_op jit(solution)/shard_map/ppermute | solution.py:308
  3.5 14.3 %all-to-all-start = ((f32[32,8,256]{2,1,0:T(8,128)}), f32[32,8,256]{2,1,0:T(8,128)S(1)}, u32[]{:S(2)}, u32[]{:S(2)}) async-start(f32[32,8,256]{2,1,0:T(8,128)} %bitcast.34), calls=%async_computation | async-start | bytes 524288 | tf_op jit(solution)/shard_map/all_to_all | solution.py:310
  14.8 0.9 copy-start
  18.8 35.5 %all-to-all-start.1 = ((f32[8,80,256]{2,1,0:T(8,128)}), f32[8,80,256]{2,1,0:T(8,128)S(1)}, u32[]{:S(2)}, u32[]{:S(2)}) async-start(f32[8,80,256]{2,1,0:T(8,128)} %pad_maximum_fusion), calls=%async_computation.1 | async-start | bytes 1310720 | tf_op jit(solution)/shard_map/all_to_all | solution.py:322
  29.5 2.4 %collective-permute-start.5 = (f32[3,256,256]{2,1,0:T(8,128)S(1)}, f32[3,256,256]{2,1,0:T(8,128)S(1)}, u32[]{:S(2)}, u32[]{:S(2)}) collective-permute-start(f32[3,256,256]{2,1,0:T(8,128)S(1)} %bitcast.39), channel_id=1, source_target_pairs={{0,1},{1,0},{2,3},{3,2},{4,5},{5,4},{6,7},{7,6},{8,9},{9,8},{10,11... | collective-permute-start | bytes 2359304 | tf_op jit(solution)/shard_map/ppermute | solution.py:304
  29.8 4.9 %collective-permute-start = (f32[3,256,256]{2,1,0:T(8,128)}, f32[3,256,256]{2,1,0:T(8,128)S(1)}, u32[]{:S(2)}, u32[]{:S(2)}) collective-permute-start(f32[3,256,256]{2,1,0:T(8,128)} %bitcast.37), channel_id=1, source_target_pairs={{0,2},{1,3},{8,10},{9,11},{16,18},{17,19},{24,26},{25,27},{32,34},... | collective-permute-start | bytes 2359304 | tf_op jit(solution)/shard_map/ppermute | solution.py:320
  30.5 23.8 %collective-permute-start.1 = (f32[3,256,256]{2,1,0:T(8,128)}, f32[3,256,256]{2,1,0:T(8,128)}, u32[]{:S(2)}, u32[]{:S(2)}) collective-permute-start(f32[3,256,256]{2,1,0:T(8,128)} %bitcast.38), channel_id=1, source_target_pairs={{0,6},{1,7},{8,14},{9,15},{16,22},{17,23},{24,30},{25,31},{32,38},... | collective-permute-start | bytes 2359304 | tf_op jit(solution)/shard_map/ppermute | solution.py:321
  31.8 59.2 %copy-start.1 = (f32[3,256,256]{2,1,0:T(8,128)}, f32[3,256,256]{2,1,0:T(8,128)S(1)}, u32[]{:S(2)}) copy-start(f32[3,256,256]{2,1,0:T(8,128)S(1)} %collective-permute-done.5) | copy-start | bytes 2359300
  31.8 46.5 %collective-permute-start.7 = (f32[3,256,256]{2,1,0:T(8,128)S(1)}, f32[3,256,256]{2,1,0:T(8,128)}, u32[]{:S(2)}, u32[]{:S(2)}) collective-permute-start(f32[3,256,256]{2,1,0:T(8,128)S(1)} %collective-permute-done.5), channel_id=1, source_target_pairs={{0,6},{1,7},{8,14},{9,15},{16,22},{17,23},{24,30},{25,31},{32,38},... | collective-permute-start | bytes 2359304 | tf_op jit(solution)/shard_map/ppermute | solution.py:326
  33.1 45.3 %collective-permute-start.6 = (f32[3,256,256]{2,1,0:T(8,128)S(1)}, f32[3,256,256]{2,1,0:T(8,128)}, u32[]{:S(2)}, u32[]{:S(2)}) collective-permute-start(f32[3,256,256]{2,1,0:T(8,128)S(1)} %collective-permute-done.5), channel_id=1, source_target_pairs={{0,2},{1,3},{8,10},{9,11},{16,18},{17,19},{24,26},{25,27},{32,34},... | collective-permute-start | bytes 2359304 | tf_op jit(solution)/shard_map/ppermute | solution.py:325
  34.7 56.3 %copy-start.2 = (f32[3,256,256]{2,1,0:T(8,128)}, f32[3,256,256]{2,1,0:T(8,128)S(1)}, u32[]{:S(2)}) copy-start(f32[3,256,256]{2,1,0:T(8,128)S(1)} %collective-permute-done) | copy-start | bytes 2359300
  34.7 43.9 %collective-permute-start.2 = (f32[3,256,256]{2,1,0:T(8,128)S(1)}, f32[3,256,256]{2,1,0:T(8,128)}, u32[]{:S(2)}, u32[]{:S(2)}) collective-permute-start(f32[3,256,256]{2,1,0:T(8,128)S(1)} %collective-permute-done), channel_id=1, source_target_pairs={{2,4},{3,5},{10,12},{11,13},{18,20},{19,21},{26,28},{27,29},{34,36... | collective-permute-start | bytes 2359304 | tf_op jit(solution)/shard_map/ppermute | solution.py:327
  55.2 23.3 %all-to-all-start.2 = ((f32[32,3,8,256]{3,2,1,0:T(8,128)}), f32[32,3,8,256]{3,2,1,0:T(8,128)S(1)}, u32[]{:S(2)}, u32[]{:S(2)}) async-start(f32[32,3,8,256]{3,2,1,0:T(8,128)} %broadcast_in_dim.26), calls=%async_computation.2 | async-start | bytes 1572864 | tf_op jit(solution)/shard_map/all_to_all | solution.py:328
  79.4 31.1 %all-to-all-start.3 = ((f32[8,2,32,256]{3,2,1,0:T(8,128)}), f32[8,2,32,256]{3,2,1,0:T(8,128)S(1)}, u32[]{:S(2)}, u32[]{:S(2)}) async-start(f32[8,2,32,256]{3,2,1,0:T(8,128)} %broadcast_in_dim.24), calls=%async_computation.3 | async-start | bytes 1048576 | tf_op jit(solution)/shard_map/all_to_all | solution.py:335
  86.6 29.5 %collective-permute-start.8 = (f32[3,256,256]{2,1,0:T(8,128)}, f32[3,256,256]{2,1,0:T(8,128)}, u32[]{:S(2)}, u32[]{:S(2)}) collective-permute-start(f32[3,256,256]{2,1,0:T(8,128)} %collective-permute-done.7), channel_id=1, source_target_pairs={{6,4},{7,5},{14,12},{15,13},{22,20},{23,21},{30,28},{31,29},{38,36... | collective-permute-start | bytes 2359304 | tf_op jit(solution)/shard_map/ppermute | solution.py:332
  112.6 18.6 %all-to-all-start.4 = ((bf16[4,256,512]{2,1,0:T(8,128)(2,1)}), bf16[4,256,512]{2,1,0:T(8,128)(2,1)S(1)}, u32[]{:S(2)}, u32[]{:S(2)}) async-start(bf16[4,256,512]{2,1,0:T(8,128)(2,1)} %right_rows.1), calls=%async_computation.4 | async-start | bytes 2097152 | tf_op jit(solution)/shard_map/all_to_all | solution.py:340
  124.1 7.0 %collective-permute-start.10 = (f32[3,256,256]{2,1,0:T(8,128)}, f32[3,256,256]{2,1,0:T(8,128)S(1)}, u32[]{:S(2)}, u32[]{:S(2)}) collective-permute-start(f32[3,256,256]{2,1,0:T(8,128)} %get-tuple-element.28), channel_id=1, source_target_pairs={{0,1},{1,0},{8,9},{9,8},{16,17},{17,16},{24,25},{25,24},{32,33},{3... | collective-permute-start | bytes 2359304 | tf_op jit(solution)/shard_map/ppermute | solution.py:349
  124.8 6.3 %collective-permute-start.9 = (bf16[3,256,512]{2,1,0:T(8,128)(2,1)}, bf16[3,256,512]{2,1,0:T(8,128)(2,1)S(1)}, u32[]{:S(2)}, u32[]{:S(2)}) collective-permute-start(bf16[3,256,512]{2,1,0:T(8,128)(2,1)} %get-tuple-element.26.both_mine), channel_id=1, source_target_pairs={{0,1},{1,0},{2,3},{3,2},{4,5},{5,4},{6,7},{7,6},{8,9},{9,8},{10,11... | collective-permute-start | bytes 2359304 | tf_op jit(solution)/shard_map/ppermute | solution.py:348

commit v3 on v2

--- a/solution.py
+++ b/solution.py
@@ -301,7 +301,6 @@
         return rows.reshape(PART, NB, NB)
 
     mine_zero = half(core)
-    other_zero = lax.ppermute(half(1 - core), "core", swapped)
 
     def place(k):
         pairs = [(zz * Y * CORE + k, zz * Y * CORE + zz) for zz in range(Z)]
@@ -317,33 +316,31 @@
         ],
         axis=1,
     )
-    mine_one = lax.ppermute(mine_zero, "y", [(0, 1)])
-    mine_three = lax.ppermute(mine_zero, "y", [(0, 3)])
+    other_zero = lax.ppermute(tie(half(1 - core), scattered), "core", swapped)
+    zero = jnp.stack([mine_zero, other_zero])
+    one = lax.ppermute(zero, "y", [(0, 1)])
+    three = lax.ppermute(zero, "y", [(0, 3)])
     from_z = lax.all_to_all(to_z, "z", 0, 0)
-    from_z = tie(from_z, mine_one, mine_three, other_zero)
     pieces = jnp.concatenate([from_z[0, :STEP], from_z[1, :2 * STEP]]).reshape(1, 3, STEP, NB)
-    other_one = lax.ppermute(other_zero, "y", [(0, 1)])
-    other_three = lax.ppermute(other_zero, "y", [(0, 3)])
-    mine_two = lax.ppermute(mine_one, "y", [(1, 2)])
     pieces = lax.all_to_all(
         jnp.broadcast_to(pieces, (X * Y * CORE, 3, STEP, NB)), PLANE, 0, 0
     )
-    pieces = tie(pieces, other_one, other_three)
-    other_two = lax.ppermute(other_three, "y", [(3, 2)])
+    pieces = tie(pieces, one, three)
+    two = lax.ppermute(one, "y", [(1, 2)])
     raw = lax.dynamic_index_in_dim(from_z[:, 2 * STEP:], column, 0).reshape(1, 2, chunk, NB)
     raw = jnp.broadcast_to(raw, (Z, 2, chunk, NB))
-    raw = lax.all_to_all(tie(raw, pieces, other_one, other_three, mine_two), "z", 0, 0)
+    raw = lax.all_to_all(tie(raw, pieces, one, three), "z", 0, 0)
 
     tables, lower, first_low = factor_leading(pieces)
 
     share = right_rows(raw, tables, first_low)
     right = lax.all_to_all(share, "x", 0, 0)
 
-    def select(zero, one, two, three):
-        return jnp.where(y == 0, zero, jnp.where(y == 1, one, jnp.where(y == 3, three, two)))
-
-    mine = select(mine_zero, mine_one, tie(mine_two, share), mine_three)
-    other = select(other_zero, other_one, tie(other_two, share), other_three)
+    zero, two = tie((zero, two), share)
+    mine, other = (
+        jnp.where(y == 0, zero[i], jnp.where(y == 1, one[i], jnp.where(y == 3, three[i], two[i])))
+        for i in range(2)
+    )
     both, keep, give = left_rows(index, mine, other, tables, lower, first_low)
     both_other = lax.ppermute(both, "core", swapped)
     lead_other = lax.ppermute(give, ("y", "core"), swapped)

time: 142 us -> 147 us (1.035)
  starting transfers between devices: 47.5 us -> 50.6 us
  other arithmetic: 3.05 us -> 5.5 us
    ppermute x7 -> x4, waiting for transfers between devices: 35.5 us -> 0.01 us  [the longest x1 0.01 us: per_device(): other_zero = lax.ppermute(tie(half(1 - core), scattered), 'core', swapped)]
    all_to_all x1, waiting for transfers between devices: 0.15 us -> 21.3 us  [per_device(): lax.all_to_all(jnp.broadcast_to(pieces, (X * Y * CORE, 3, STEP, NB)), PLA...]
    all_to_all x1, waiting for transfers between devices: 0.01 us -> 14.1 us  [per_device(): from_z = lax.all_to_all(to_z, 'z', 0, 0)]
    all_to_all x1, starting transfers between devices: 10.6 us -> 18.7 us  [per_device(): from_z = lax.all_to_all(to_z, 'z', 0, 0)]
    ppermute x7 -> x4, starting transfers between devices: 11.1 us -> 5.4 us  [the longest x1 1.83 us: per_device(): two = lax.ppermute(one, 'y', [(1, 2)])]
    all_to_all x1, waiting for transfers between devices: 1.26 us -> 3.02 us  [per_device(): lax.all_to_all(top.reshape(X * Y * CORE, STEP, NB), PLANE, 0, 0)[:2]]
  transfers between devices with their start and end apart: 16 -> 13, of which waited for: 6 -> 4; matrix products, arithmetic and copies ran while one was open for 6% -> 8% of each run, Pallas kernels for 19% -> 19%
where the time goes in v3:
time: 147 us; the launch traced here: 146 us
  starting transfers between devices  50.6 us (34%)
  waiting for transfers between devices  43.9 us (30%)
  Pallas kernels  37.2 us (25%)
  local copies, waits for them, and re-layouts  8.88 us (6%)
  other arithmetic  5.5 us (4%)
    all_to_all x1, waiting for transfers between devices, per_device(): lax.all_to_all(jnp.broadcast_to(pieces, (X * Y * CORE, 3, STEP, NB)), PLA...  21.3 us
    pallas_call x1, Pallas kernels, factor_leading(): pl.pallas_call(leading_kernel, out_shape=[jax.ShapeDtypeStruct((2, 6 * NB...  19.4 us
    all_to_all x1, starting transfers between devices, per_device(): from_z = lax.all_to_all(to_z, 'z', 0, 0)  18.7 us
    all_to_all x1, waiting for transfers between devices, per_device(): from_z = lax.all_to_all(to_z, 'z', 0, 0)  14.1 us
    pallas_call x1, Pallas kernels, update(): pl.pallas_call(update_kernel, grid_spec=pltpu.PrefetchScalarGridSpec(num_...  9.74 us
    all_to_all x1, starting transfers between devices, per_device(): lax.all_to_all(top.reshape(X * Y * CORE, STEP, NB), PLANE, 0, 0)[:2]  7.31 us
    all_to_all x1, starting transfers between devices, per_device(): raw = lax.all_to_all(tie(raw, pieces, one, three), 'z', 0, 0)  6.93 us
    all_to_all x1, starting transfers between devices, per_device(): lax.all_to_all(jnp.broadcast_to(pieces, (X * Y * CORE, 3, STEP, NB)), PLA...  6.64 us
  transfers between devices with their start and end apart: 13, of which 4 were waited for; matrix products, arithmetic and copies ran while one was open for 8% of the time, Pallas kernels for 19%

profile of v3, /device:TPU:24, one launch (start us, length us, event | category | flops | bytes accessed | tf_op | source)
XLA Modules:
  0.0 146.3 jit_solution(17755895655694861407)
XLA Ops:
  0.0 1.4 slice.39
  1.4 0.7 copy.16
  2.1 7.3 %all-to-all-start = ((f32[32,8,256]{2,1,0:T(8,128)}), f32[32,8,256]{2,1,0:T(8,128)S(1)}, u32[]{:S(2)}, u32[]{:S(2)}) async-start(f32[32,8,256]{2,1,0:T(8,128)} %bitcast.31.clone.2), calls=%async_computation | async-start | bytes 524288 | tf_op jit(solution)/shard_map/all_to_all | solution.py:309
  9.5 3.9 %constant_dynamic-slice_fusion.2 = (f32[3,256,1,256]{3,2,1,0:T(1,128)S(1)}, f32[3,256,1,256]{3,2,1,0:T(1,128)S(1)}) fusion(f32[6,256,4,256]{3,2,1,0:T(4,128)} %param.1, s32[]{:T(128)S(6)} %select_n.51, s32[]{:T(128)S(6)} %select_n.52), kind=kLoop, calls=%fused_computation.20 | loop fusion | bytes 3145736 | tf_op jit(solution)/shard_map/dynamic_slice | solution.py:300
  13.4 0.1 copy.14
  13.4 3.0 %all-to-all-done = f32[32,8,256]{2,1,0:T(8,128)S(1)} async-done(((f32[32,8,256]{2,1,0:T(8,128)}), f32[32,8,256]{2,1,0:T(8,128)S(1)}, u32[]{:S(2)}, u32[]{:S(2)}) %all-to-all-start) | async-done | bytes 262176 | tf_op jit(solution)/shard_map/all_to_all | solution.py:309
  16.5 0.5 collective-permute-start
  17.0 0.7 collective-permute-start.3
  17.6 0.7 collective-permute-start.4
  18.4 0.9 pad_maximum_fusion.1
  19.3 18.7 %all-to-all-start.1 = ((f32[8,80,256]{2,1,0:T(8,128)}), f32[8,80,256]{2,1,0:T(8,128)S(1)}, u32[]{:S(2)}, u32[]{:S(2)}) async-start(f32[8,80,256]{2,1,0:T(8,128)} %pad_maximum_fusion.1), calls=%async_computation.1 | async-start | bytes 1310720 | tf_op jit(solution)/shard_map/all_to_all | solution.py:323
  38.1 0.9 copy-done.1
  38.9 1.3 pad_maximum_fusion
  40.2 1.8 %collective-permute-start.1 = (f32[2,3,256,256]{3,2,1,0:T(8,128)S(1)}, f32[2,3,256,256]{3,2,1,0:T(8,128)}, u32[]{:S(2)}, u32[]{:S(2)}) collective-permute-start(f32[2,3,256,256]{3,2,1,0:T(8,128)S(1)} %pad_maximum_fusion), channel_id=1, source_target_pairs={{0,2},{1,3},{8,10},{9,11},{16,18},{17,19},{24,26},{25,27},{32,34},... | collective-permute-start | bytes 4718600 | tf_op jit(solution)/shard_map/ppermute | solution.py:321
  42.0 1.3 collective-permute-start.5
  43.3 14.1 %all-to-all-done.1 = f32[8,80,256]{2,1,0:T(8,128)S(1)} async-done(((f32[8,80,256]{2,1,0:T(8,128)}), f32[8,80,256]{2,1,0:T(8,128)S(1)}, u32[]{:S(2)}, u32[]{:S(2)}) %all-to-all-start.1) | async-done | bytes 655392 | tf_op jit(solution)/shard_map/all_to_all | solution.py:323
  57.5 0.9 broadcast_in_dim.26
  58.4 6.6 %all-to-all-start.2 = ((f32[32,3,8,256]{3,2,1,0:T(8,128)}), f32[32,3,8,256]{3,2,1,0:T(8,128)S(1)}, u32[]{:S(2)}, u32[]{:S(2)}) async-start(f32[32,3,8,256]{3,2,1,0:T(8,128)} %broadcast_in_dim.26), calls=%async_computation.2 | async-start | bytes 1572864 | tf_op jit(solution)/shard_map/all_to_all | solution.py:325
  65.1 1.8 %collective-permute-start.2 = (f32[2,3,256,256]{3,2,1,0:T(8,128)}, f32[2,3,256,256]{3,2,1,0:T(8,128)}, u32[]{:S(2)}, u32[]{:S(2)}) collective-permute-start(f32[2,3,256,256]{3,2,1,0:T(8,128)} %collective-permute-done.1), channel_id=1, source_target_pairs={{2,4},{3,5},{10,12},{11,13},{18,20},{19,21},{26,28},{27,29},{34,36... | collective-permute-start | bytes 4718600 | tf_op jit(solution)/shard_map/ppermute | solution.py:329
  67.0 21.3 %all-to-all-done.2.pieces = f32[32,3,8,256]{3,2,1,0:T(8,128)S(1)} async-done(((f32[32,3,8,256]{3,2,1,0:T(8,128)}), f32[32,3,8,256]{3,2,1,0:T(8,128)S(1)}, u32[]{:S(2)}, u32[]{:S(2)}) %all-to-all-start.2) | async-done | bytes 786464 | tf_op jit(solution)/shard_map/all_to_all | solution.py:325
  88.3 0.8 broadcast_in_dim.24
  89.1 6.9 %all-to-all-start.3 = ((f32[8,2,32,256]{3,2,1,0:T(8,128)}), f32[8,2,32,256]{3,2,1,0:T(8,128)S(1)}, u32[]{:S(2)}, u32[]{:S(2)}) async-start(f32[8,2,32,256]{3,2,1,0:T(8,128)} %broadcast_in_dim.24), calls=%async_computation.3 | async-start | bytes 1048576 | tf_op jit(solution)/shard_map/all_to_all | solution.py:332
  96.1 0.1 pad_add_fusion.index
  96.1 19.4 %leading.1 = (bf16[2,1536,256]{2,1,0:T(8,128)(2,1)S(1)}, f32[2,256,256]{2,1,0:T(8,128)}, bf16[256,256]{1,0:T(8,128)(2,1)S(1)}) custom-call(f32[32,3,8,256]{3,2,1,0:T(8,128)S(1)} %all-to-all-done.2.pieces), custom_call_target="tpu_custom_call" | custom-call | flops 1024 | bytes 1024 | tf_op jit(solution)/shard_map/leading/pallas_call | solution.py:157
  115.5 2.1 %right_rows.1 = bf16[4,256,512]{2,1,0:T(8,128)(2,1)} custom-call(f32[8,2,32,256]{3,2,1,0:T(8,128)S(1)} %all-to-all-done.3.raw, bf16[2,1536,256]{2,1,0:T(8,128)(2,1)S(1)} %get-tuple-element.19.tables, bf16[256,256]{1,0:T(8,128)(2,1)S(1)} %get-tuple-element.20.first_low), custom_call_target="tpu_custom_call" | custom-call | flops 1024 | bytes 1024 | tf_op jit(solution)/shard_map/right_rows/pallas_call | solution.py:231
  117.6 3.5 %all-to-all-start.4 = ((bf16[4,256,512]{2,1,0:T(8,128)(2,1)}), bf16[4,256,512]{2,1,0:T(8,128)(2,1)S(1)}, u32[]{:S(2)}, u32[]{:S(2)}) async-start(bf16[4,256,512]{2,1,0:T(8,128)(2,1)} %right_rows.1), calls=%async_computation.4 | async-start | bytes 2097152 | tf_op jit(solution)/shard_map/all_to_all | solution.py:337
  121.2 3.2 %fusion.2 = (f32[3,256,256]{2,1,0:T(8,128)S(1)}, f32[3,256,256]{2,1,0:T(8,128)S(1)}) fusion(f32[2,3,256,256]{3,2,1,0:T(8,128)} %collective-permute-done.5, f32[2,3,256,256]{3,2,1,0:T(8,128)} %collective-permute-done.1, f32[2,3,256,256]{3,2,1,0:T(8,128)} %collective-permute-done.2, f32[2,3,256,256]{3,2,1,0:T(8,128)} %copy-done, pred[]{:T(512)S(6)} %eq.14, ...), kind=kLoop, calls=%fused_computation.4 | loop fusion | flops 1179648 | bytes 7864323 | tf_op jit(solution)/shard_map/jit(_where)/select_n | solution.py:341
  124.4 5.9 %left_rows.1 = (bf16[3,256,512]{2,1,0:T(8,128)(2,1)}, f32[3,256,256]{2,1,0:T(8,128)}, f32[3,256,256]{2,1,0:T(8,128)}) custom-call(s32[3]{0:T(128)S(1)} %pad_add_fusion.index, f32[3,256,256]{2,1,0:T(8,128)S(1)} %get-tuple-element.28.mine, f32[3,256,256]{2,1,0:T(8,128)S(1)} %get-tuple-element.27.other, bf16[2,1536,256]{2,1,0:T(8,128)(2,1)S(1)} %get-tuple-element.19.tables, ...), custom_call_target="tpu_custom_call" | custom-call | flops 1024 | bytes 1024 | tf_op jit(solution)/shard_map/left_rows/pallas_call | solution.py:205
  130.3 0.7 collective-permute-start.7
  131.0 0.1 collective-permute-start.6
  131.1 5.4 %all-to-all-done.4.right = bf16[4,256,512]{2,1,0:T(8,128)(2,1)S(1)} async-done(((bf16[4,256,512]{2,1,0:T(8,128)(2,1)}), bf16[4,256,512]{2,1,0:T(8,128)(2,1)S(1)}, u32[]{:S(2)}, u32[]{:S(2)}) %all-to-all-start.4) | async-done | bytes 1048608 | tf_op jit(solution)/shard_map/all_to_all | solution.py:337
  136.5 9.7 %update.1 = f32[2,3,256,4,256]{4,3,2,1,0:T(4,128)} custom-call(s32[3]{0:T(128)S(1)} %pad_add_fusion.index, f32[2,3,256,4,256]{4,3,2,1,0:T(4,128)} %bitcast.38, bf16[3,256,512]{2,1,0:T(8,128)(2,1)} %get-tuple-element.24.both_mine, bf16[3,256,512]{2,1,0:T(8,128)(2,1)S(1)} %collective-permute-done.6.both_other, f32[3,256,256]{2,1,0:T(8,128)} %get-tuple-element.25.lead_mine, ...), custom_call_target="tpu_custom_call" | custom-call | flops 1024 | bytes 1024 | tf_op jit(solution)/shard_map/update/pallas_call | solution.py:261
  (21 shorter events, 0.2 us)
Async XLA Ops:
  2.1 14.3 %all-to-all-start = ((f32[32,8,256]{2,1,0:T(8,128)}), f32[32,8,256]{2,1,0:T(8,128)S(1)}, u32[]{:S(2)}, u32[]{:S(2)}) async-start(f32[32,8,256]{2,1,0:T(8,128)} %bitcast.31.clone.2), calls=%async_computation | async-start | bytes 524288 | tf_op jit(solution)/shard_map/all_to_all | solution.py:309
  16.5 21.6 %collective-permute-start = (f32[3,256,256]{2,1,0:T(8,128)S(1)}, f32[3,256,256]{2,1,0:T(8,128)S(1)}, u32[]{:S(2)}, u32[]{:S(2)}) collective-permute-start(f32[3,256,256]{2,1,0:T(8,128)S(1)} %bitcast.41), channel_id=1, source_target_pairs={{0,1},{1,0},{2,3},{3,2},{4,5},{5,4},{6,7},{7,6},{8,9},{9,8},{10,11... | collective-permute-start | bytes 2359304 | tf_op jit(solution)/shard_map/ppermute | solution.py:319
  17.0 1.4 collective-permute-start.3
  17.6 0.7 collective-permute-start.4
  19.3 38.1 %all-to-all-start.1 = ((f32[8,80,256]{2,1,0:T(8,128)}), f32[8,80,256]{2,1,0:T(8,128)S(1)}, u32[]{:S(2)}, u32[]{:S(2)}) async-start(f32[8,80,256]{2,1,0:T(8,128)} %pad_maximum_fusion.1), calls=%async_computation.1 | async-start | bytes 1310720 | tf_op jit(solution)/shard_map/all_to_all | solution.py:323
  38.0 0.9 copy-start.1
  40.2 26.7 %copy-start = (f32[2,3,256,256]{3,2,1,0:T(8,128)}, f32[2,3,256,256]{3,2,1,0:T(8,128)S(1)}, u32[]{:S(2)}) copy-start(f32[2,3,256,256]{3,2,1,0:T(8,128)S(1)} %pad_maximum_fusion) | copy-start | bytes 4718596
  40.2 24.8 %collective-permute-start.1 = (f32[2,3,256,256]{3,2,1,0:T(8,128)S(1)}, f32[2,3,256,256]{3,2,1,0:T(8,128)}, u32[]{:S(2)}, u32[]{:S(2)}) collective-permute-start(f32[2,3,256,256]{3,2,1,0:T(8,128)S(1)} %pad_maximum_fusion), channel_id=1, source_target_pairs={{0,2},{1,3},{8,10},{9,11},{16,18},{17,19},{24,26},{25,27},{32,34},... | collective-permute-start | bytes 4718600 | tf_op jit(solution)/shard_map/ppermute | solution.py:321
  42.0 46.3 %collective-permute-start.5 = (f32[2,3,256,256]{3,2,1,0:T(8,128)S(1)}, f32[2,3,256,256]{3,2,1,0:T(8,128)}, u32[]{:S(2)}, u32[]{:S(2)}) collective-permute-start(f32[2,3,256,256]{3,2,1,0:T(8,128)S(1)} %pad_maximum_fusion), channel_id=1, source_target_pairs={{0,6},{1,7},{8,14},{9,15},{16,22},{17,23},{24,30},{25,31},{32,38},... | collective-permute-start | bytes 4718600 | tf_op jit(solution)/shard_map/ppermute | solution.py:322
  58.4 29.9 %all-to-all-start.2 = ((f32[32,3,8,256]{3,2,1,0:T(8,128)}), f32[32,3,8,256]{3,2,1,0:T(8,128)S(1)}, u32[]{:S(2)}, u32[]{:S(2)}) async-start(f32[32,3,8,256]{3,2,1,0:T(8,128)} %broadcast_in_dim.26), calls=%async_computation.2 | async-start | bytes 1572864 | tf_op jit(solution)/shard_map/all_to_all | solution.py:325
  65.1 56.1 %collective-permute-start.2 = (f32[2,3,256,256]{3,2,1,0:T(8,128)}, f32[2,3,256,256]{3,2,1,0:T(8,128)}, u32[]{:S(2)}, u32[]{:S(2)}) collective-permute-start(f32[2,3,256,256]{3,2,1,0:T(8,128)} %collective-permute-done.1), channel_id=1, source_target_pairs={{2,4},{3,5},{10,12},{11,13},{18,20},{19,21},{26,28},{27,29},{34,36... | collective-permute-start | bytes 4718600 | tf_op jit(solution)/shard_map/ppermute | solution.py:329
  89.1 26.4 %all-to-all-start.3 = ((f32[8,2,32,256]{3,2,1,0:T(8,128)}), f32[8,2,32,256]{3,2,1,0:T(8,128)S(1)}, u32[]{:S(2)}, u32[]{:S(2)}) async-start(f32[8,2,32,256]{3,2,1,0:T(8,128)} %broadcast_in_dim.24), calls=%async_computation.3 | async-start | bytes 1048576 | tf_op jit(solution)/shard_map/all_to_all | solution.py:332
  117.6 18.9 %all-to-all-start.4 = ((bf16[4,256,512]{2,1,0:T(8,128)(2,1)}), bf16[4,256,512]{2,1,0:T(8,128)(2,1)S(1)}, u32[]{:S(2)}, u32[]{:S(2)}) async-start(bf16[4,256,512]{2,1,0:T(8,128)(2,1)} %right_rows.1), calls=%async_computation.4 | async-start | bytes 2097152 | tf_op jit(solution)/shard_map/all_to_all | solution.py:337
  130.3 6.2 %collective-permute-start.7 = (f32[3,256,256]{2,1,0:T(8,128)}, f32[3,256,256]{2,1,0:T(8,128)S(1)}, u32[]{:S(2)}, u32[]{:S(2)}) collective-permute-start(f32[3,256,256]{2,1,0:T(8,128)} %get-tuple-element.26), channel_id=1, source_target_pairs={{0,1},{1,0},{8,9},{9,8},{16,17},{17,16},{24,25},{25,24},{32,33},{3... | collective-permute-start | bytes 2359304 | tf_op jit(solution)/shard_map/ppermute | solution.py:346
  131.0 5.5 %collective-permute-start.6 = (bf16[3,256,512]{2,1,0:T(8,128)(2,1)}, bf16[3,256,512]{2,1,0:T(8,128)(2,1)S(1)}, u32[]{:S(2)}, u32[]{:S(2)}) collective-permute-start(bf16[3,256,512]{2,1,0:T(8,128)(2,1)} %get-tuple-element.24.both_mine), channel_id=1, source_target_pairs={{0,1},{1,0},{2,3},{3,2},{4,5},{5,4},{6,7},{7,6},{8,9},{9,8},{10,11... | collective-permute-start | bytes 2359304 | tf_op jit(solution)/shard_map/ppermute | solution.py:345

commit v4 on v2

--- a/solution.py
+++ b/solution.py
@@ -241,16 +241,19 @@
 
 def update_kernel(index, slab, both_mine, both_other, lead_mine, lead_other, right, out):
     col_index = index[1]
-    for part in range(2):
-        own = index[2] == part
-        row_block = (part * PART + pl.program_id(0)) * (X * Z) + index[0]
-        both = jnp.where(own, both_mine[0], both_other[0])
-        for m in range(CBL):
-            change = times_transposed(both, right[m])
+    swap = index[2] == 1
+    both = jnp.concatenate(
+        [jnp.where(swap, both_other[0], both_mine[0]), jnp.where(swap, both_mine[0], both_other[0])]
+    )
+    for m in range(CBL):
+        change = times_transposed(both, right[m])
+        for part in range(2):
+            row_block = (part * PART + pl.program_id(0)) * (X * Z) + index[0]
             live = (row_block >= 2) & (m * (Y * CORE) + col_index >= 2)
-            value = slab[part, 0, :, m, :] - jnp.where(live, change, 0.0)
+            rows = change[part * NB:(part + 1) * NB]
+            value = slab[part, 0, :, m, :] - jnp.where(live, rows, 0.0)
             if m == 0:
-                lead = jnp.where(own, lead_mine[0], lead_other[0])
+                lead = jnp.where(index[2] == part, lead_mine[0], lead_other[0])
                 value = jnp.where(col_index < 2, lead, value)
             out[part, 0, :, m, :] = value
 

time: 142 us -> 142 us (level)
  no operation moved by 1% of the time
where the time goes in v4:
time: 142 us; the launch traced here: 141 us
  starting transfers between devices  47.5 us (33%)
  waiting for transfers between devices  43.2 us (30%)
  Pallas kernels  37.2 us (26%)
  local copies, waits for them, and re-layouts  9.77 us (7%)
  other arithmetic  3.05 us (2%)
    pallas_call x1, Pallas kernels, factor_leading(): pl.pallas_call(leading_kernel, out_shape=[jax.ShapeDtypeStruct((2, 6 * NB...  19.4 us
    ppermute x1, waiting for transfers between devices, per_device(): mine_three = lax.ppermute(mine_zero, 'y', [(0, 3)])  18 us
    ppermute x1, waiting for transfers between devices, per_device(): other_three = lax.ppermute(other_zero, 'y', [(0, 3)])  17.5 us
    all_to_all x1, starting transfers between devices, per_device(): from_z = lax.all_to_all(to_z, 'z', 0, 0)  10.6 us
    pallas_call x1, Pallas kernels, update(): pl.pallas_call(update_kernel, grid_spec=pltpu.PrefetchScalarGridSpec(num_...  9.78 us
    all_to_all x1, starting transfers between devices, per_device(): lax.all_to_all(top.reshape(X * Y * CORE, STEP, NB), PLANE, 0, 0)[:2]  7.32 us
    all_to_all x1, starting transfers between devices, per_device(): lax.all_to_all(tie(raw, pieces, other_one, other_three, mine_two), 'z', 0...  7.21 us
    all_to_all x1, waiting for transfers between devices, per_device(): right = lax.all_to_all(share, 'x', 0, 0)  6.23 us
  transfers between devices with their start and end apart: 16, of which 6 were waited for; matrix products, arithmetic and copies ran while one was open for 6% of the time, Pallas kernels for 19%

profile of v4, /device:TPU:24, one launch (start us, length us, event | category | flops | bytes accessed | tf_op | source)
XLA Modules:
  0.0 140.9 jit_solution(11600202166483635884)
XLA Ops:
  0.0 1.4 slice.15
  1.4 0.7 copy.18
  2.1 0.7 collective-permute-start.3
  2.8 0.7 collective-permute-start.4
  3.5 7.3 %all-to-all-start = ((f32[32,8,256]{2,1,0:T(8,128)}), f32[32,8,256]{2,1,0:T(8,128)S(1)}, u32[]{:S(2)}, u32[]{:S(2)}) async-start(f32[32,8,256]{2,1,0:T(8,128)} %bitcast.34), calls=%async_computation | async-start | bytes 524288 | tf_op jit(solution)/shard_map/all_to_all | solution.py:313
  10.8 3.9 %constant_dynamic-slice_fusion.1 = (f32[3,256,1,256]{3,2,1,0:T(1,128)S(1)}, f32[3,256,1,256]{3,2,1,0:T(1,128)S(1)}) fusion(f32[6,256,4,256]{3,2,1,0:T(4,128)} %param.1, s32[]{:T(128)S(6)} %select_n.46, s32[]{:T(128)S(6)} %select_n.43), kind=kLoop, calls=%fused_computation.12 | loop fusion | bytes 3145736 | tf_op jit(solution)/shard_map/dynamic_slice | solution.py:303
  14.8 0.9 copy-done
  15.6 0.9 copy.17
  16.6 1.3 all-to-all-done
  17.9 0.9 pad_maximum_fusion
  18.8 10.6 %all-to-all-start.1 = ((f32[8,80,256]{2,1,0:T(8,128)}), f32[8,80,256]{2,1,0:T(8,128)S(1)}, u32[]{:S(2)}, u32[]{:S(2)}) async-start(f32[8,80,256]{2,1,0:T(8,128)} %pad_maximum_fusion), calls=%async_computation.1 | async-start | bytes 1310720 | tf_op jit(solution)/shard_map/all_to_all | solution.py:325
  29.5 0.3 collective-permute-start.5
  29.8 0.7 collective-permute-start
  30.5 1.3 collective-permute-start.1
  31.8 1.3 collective-permute-start.7
  33.1 1.6 %collective-permute-start.6 = (f32[3,256,256]{2,1,0:T(8,128)S(1)}, f32[3,256,256]{2,1,0:T(8,128)}, u32[]{:S(2)}, u32[]{:S(2)}) collective-permute-start(f32[3,256,256]{2,1,0:T(8,128)S(1)} %collective-permute-done.5), channel_id=1, source_target_pairs={{0,2},{1,3},{8,10},{9,11},{16,18},{17,19},{24,26},{25,27},{32,34},... | collective-permute-start | bytes 2359304 | tf_op jit(solution)/shard_map/ppermute | solution.py:328
  34.7 1.6 %collective-permute-start.2 = (f32[3,256,256]{2,1,0:T(8,128)S(1)}, f32[3,256,256]{2,1,0:T(8,128)}, u32[]{:S(2)}, u32[]{:S(2)}) collective-permute-start(f32[3,256,256]{2,1,0:T(8,128)S(1)} %collective-permute-done), channel_id=1, source_target_pairs={{2,4},{3,5},{10,12},{11,13},{18,20},{19,21},{26,28},{27,29},{34,36... | collective-permute-start | bytes 2359304 | tf_op jit(solution)/shard_map/ppermute | solution.py:330
  36.3 18.0 %collective-permute-done.1 = f32[3,256,256]{2,1,0:T(8,128)} collective-permute-done((f32[3,256,256]{2,1,0:T(8,128)}, f32[3,256,256]{2,1,0:T(8,128)}, u32[]{:S(2)}, u32[]{:S(2)}) %collective-permute-start.1) | collective-permute-done | bytes 786464 | tf_op jit(solution)/shard_map/ppermute | solution.py:324
  54.3 0.9 broadcast_in_dim.26
  55.2 5.6 %all-to-all-start.2 = ((f32[32,3,8,256]{3,2,1,0:T(8,128)}), f32[32,3,8,256]{3,2,1,0:T(8,128)S(1)}, u32[]{:S(2)}, u32[]{:S(2)}) async-start(f32[32,3,8,256]{3,2,1,0:T(8,128)} %broadcast_in_dim.26), calls=%async_computation.2 | async-start | bytes 1572864 | tf_op jit(solution)/shard_map/all_to_all | solution.py:331
  60.9 17.5 %collective-permute-done.7 = f32[3,256,256]{2,1,0:T(8,128)} collective-permute-done((f32[3,256,256]{2,1,0:T(8,128)S(1)}, f32[3,256,256]{2,1,0:T(8,128)}, u32[]{:S(2)}, u32[]{:S(2)}) %collective-permute-start.7) | collective-permute-done | bytes 786464 | tf_op jit(solution)/shard_map/ppermute | solution.py:329
  78.6 0.8 broadcast_in_dim.24
  79.4 7.2 %all-to-all-start.3 = ((f32[8,2,32,256]{3,2,1,0:T(8,128)}), f32[8,2,32,256]{3,2,1,0:T(8,128)S(1)}, u32[]{:S(2)}, u32[]{:S(2)}) async-start(f32[8,2,32,256]{3,2,1,0:T(8,128)} %broadcast_in_dim.24), calls=%async_computation.3 | async-start | bytes 1048576 | tf_op jit(solution)/shard_map/all_to_all | solution.py:338
  86.6 4.4 %collective-permute-start.8 = (f32[3,256,256]{2,1,0:T(8,128)}, f32[3,256,256]{2,1,0:T(8,128)}, u32[]{:S(2)}, u32[]{:S(2)}) collective-permute-start(f32[3,256,256]{2,1,0:T(8,128)} %collective-permute-done.7), channel_id=1, source_target_pairs={{6,4},{7,5},{14,12},{15,13},{22,20},{23,21},{30,28},{31,29},{38,36... | collective-permute-start | bytes 2359304 | tf_op jit(solution)/shard_map/ppermute | solution.py:335
  91.1 19.4 %leading.1 = (bf16[2,1536,256]{2,1,0:T(8,128)(2,1)S(1)}, f32[2,256,256]{2,1,0:T(8,128)}, bf16[256,256]{1,0:T(8,128)(2,1)S(1)}) custom-call(f32[32,3,8,256]{3,2,1,0:T(8,128)S(1)} %all-to-all-done.2.pieces), custom_call_target="tpu_custom_call" | custom-call | flops 1024 | bytes 1024 | tf_op jit(solution)/shard_map/leading/pallas_call | solution.py:157
  110.5 2.1 %right_rows.1 = bf16[4,256,512]{2,1,0:T(8,128)(2,1)} custom-call(f32[8,2,32,256]{3,2,1,0:T(8,128)S(1)} %all-to-all-done.3.raw, bf16[2,1536,256]{2,1,0:T(8,128)(2,1)S(1)} %get-tuple-element.21.tables, bf16[256,256]{1,0:T(8,128)(2,1)S(1)} %get-tuple-element.22.first_low), custom_call_target="tpu_custom_call" | custom-call | flops 1024 | bytes 1024 | tf_op jit(solution)/shard_map/right_rows/pallas_call | solution.py:231
  112.6 3.5 %all-to-all-start.4 = ((bf16[4,256,512]{2,1,0:T(8,128)(2,1)}), bf16[4,256,512]{2,1,0:T(8,128)(2,1)S(1)}, u32[]{:S(2)}, u32[]{:S(2)}) async-start(bf16[4,256,512]{2,1,0:T(8,128)(2,1)} %right_rows.1), calls=%async_computation.4 | async-start | bytes 2097152 | tf_op jit(solution)/shard_map/all_to_all | solution.py:343
  116.1 2.0 %select_select_fusion = (f32[3,256,256]{2,1,0:T(8,128)S(1)}, f32[3,256,256]{2,1,0:T(8,128)S(1)}) fusion(f32[3,256,256]{2,1,0:T(8,128)} %copy-done.1, f32[3,256,256]{2,1,0:T(8,128)} %collective-permute-done.6, f32[3,256,256]{2,1,0:T(8,128)} %collective-permute-done.7, f32[3,256,256]{2,1,0:T(8,128)} %collective-permute-done.8, pred[]{:T(512)S(6)} %eq.14, ...), kind=kLoop, calls=%fused_computation.2 | loop fusion | flops 1179648 | bytes 7864323 | tf_op jit(solution)/shard_map/jit(_where)/select_n | solution.py:346
  118.1 6.0 %left_rows.1 = (bf16[3,256,512]{2,1,0:T(8,128)(2,1)}, f32[3,256,256]{2,1,0:T(8,128)}, f32[3,256,256]{2,1,0:T(8,128)}) custom-call(s32[3]{0:T(128)S(1)} %pad_add_fusion.index, f32[3,256,256]{2,1,0:T(8,128)S(1)} %get-tuple-element.34.mine, f32[3,256,256]{2,1,0:T(8,128)S(1)} %get-tuple-element.33.other, bf16[2,1536,256]{2,1,0:T(8,128)(2,1)S(1)} %get-tuple-element.21.tables, ...), custom_call_target="tpu_custom_call" | custom-call | flops 1024 | bytes 1024 | tf_op jit(solution)/shard_map/left_rows/pallas_call | solution.py:205
  124.1 0.7 collective-permute-start.10
  124.9 6.2 %all-to-all-done.4.right = bf16[4,256,512]{2,1,0:T(8,128)(2,1)S(1)} async-done(((bf16[4,256,512]{2,1,0:T(8,128)(2,1)}), bf16[4,256,512]{2,1,0:T(8,128)(2,1)S(1)}, u32[]{:S(2)}, u32[]{:S(2)}) %all-to-all-start.4) | async-done | bytes 1048608 | tf_op jit(solution)/shard_map/all_to_all | solution.py:343
  131.1 9.8 %update.1 = f32[2,3,256,4,256]{4,3,2,1,0:T(4,128)} custom-call(s32[3]{0:T(128)S(1)} %pad_add_fusion.index, f32[2,3,256,4,256]{4,3,2,1,0:T(4,128)} %bitcast.35, bf16[3,256,512]{2,1,0:T(8,128)(2,1)} %get-tuple-element.26.both_mine, bf16[3,256,512]{2,1,0:T(8,128)(2,1)S(1)} %collective-permute-done.9.both_other, f32[3,256,256]{2,1,0:T(8,128)} %get-tuple-element.27.lead_mine, ...), custom_call_target="tpu_custom_call" | custom-call | flops 1024 | bytes 1024 | tf_op jit(solution)/shard_map/update/pallas_call | solution.py:264
  (28 shorter events, 0.6 us)
Async XLA Ops:
  2.1 15.7 %collective-permute-start.3 = (f32[256,256]{1,0:T(8,128)}, f32[256,256]{1,0:T(8,128)S(1)}, u32[]{:S(2)}, u32[]{:S(2)}) collective-permute-start(f32[256,256]{1,0:T(8,128)} %bitcast.25.clone.2), channel_id=1, source_target_pairs={{0,0},{8,9},{16,18},{24,27},{32,36},{40,45},{48,54},{56,63},{64,64... | collective-permute-start | bytes 786440 | tf_op jit(solution)/shard_map/ppermute | solution.py:311
  2.8 15.0 %collective-permute-start.4 = (f32[256,256]{1,0:T(8,128)}, f32[256,256]{1,0:T(8,128)S(1)}, u32[]{:S(2)}, u32[]{:S(2)}) collective-permute-start(f32[256,256]{1,0:T(8,128)} %bitcast.25.clone.2), channel_id=1, source_target_pairs={{1,0},{9,9},{17,18},{25,27},{33,36},{41,45},{49,54},{57,63},{65,64... | collective-permute-start | bytes 786440 | tf_op jit(solution)/shard_map/ppermute | solution.py:311
  3.5 14.3 %all-to-all-start = ((f32[32,8,256]{2,1,0:T(8,128)}), f32[32,8,256]{2,1,0:T(8,128)S(1)}, u32[]{:S(2)}, u32[]{:S(2)}) async-start(f32[32,8,256]{2,1,0:T(8,128)} %bitcast.34), calls=%async_computation | async-start | bytes 524288 | tf_op jit(solution)/shard_map/all_to_all | solution.py:313
  14.8 0.9 copy-start
  18.8 35.5 %all-to-all-start.1 = ((f32[8,80,256]{2,1,0:T(8,128)}), f32[8,80,256]{2,1,0:T(8,128)S(1)}, u32[]{:S(2)}, u32[]{:S(2)}) async-start(f32[8,80,256]{2,1,0:T(8,128)} %pad_maximum_fusion), calls=%async_computation.1 | async-start | bytes 1310720 | tf_op jit(solution)/shard_map/all_to_all | solution.py:325
  29.5 2.4 %collective-permute-start.5 = (f32[3,256,256]{2,1,0:T(8,128)S(1)}, f32[3,256,256]{2,1,0:T(8,128)S(1)}, u32[]{:S(2)}, u32[]{:S(2)}) collective-permute-start(f32[3,256,256]{2,1,0:T(8,128)S(1)} %bitcast.39), channel_id=1, source_target_pairs={{0,1},{1,0},{2,3},{3,2},{4,5},{5,4},{6,7},{7,6},{8,9},{9,8},{10,11... | collective-permute-start | bytes 2359304 | tf_op jit(solution)/shard_map/ppermute | solution.py:307
  29.8 4.9 %collective-permute-start = (f32[3,256,256]{2,1,0:T(8,128)}, f32[3,256,256]{2,1,0:T(8,128)S(1)}, u32[]{:S(2)}, u32[]{:S(2)}) collective-permute-start(f32[3,256,256]{2,1,0:T(8,128)} %bitcast.37), channel_id=1, source_target_pairs={{0,2},{1,3},{8,10},{9,11},{16,18},{17,19},{24,26},{25,27},{32,34},... | collective-permute-start | bytes 2359304 | tf_op jit(solution)/shard_map/ppermute | solution.py:323
  30.5 23.8 %collective-permute-start.1 = (f32[3,256,256]{2,1,0:T(8,128)}, f32[3,256,256]{2,1,0:T(8,128)}, u32[]{:S(2)}, u32[]{:S(2)}) collective-permute-start(f32[3,256,256]{2,1,0:T(8,128)} %bitcast.38), channel_id=1, source_target_pairs={{0,6},{1,7},{8,14},{9,15},{16,22},{17,23},{24,30},{25,31},{32,38},... | collective-permute-start | bytes 2359304 | tf_op jit(solution)/shard_map/ppermute | solution.py:324
  31.8 59.2 %copy-start.1 = (f32[3,256,256]{2,1,0:T(8,128)}, f32[3,256,256]{2,1,0:T(8,128)S(1)}, u32[]{:S(2)}) copy-start(f32[3,256,256]{2,1,0:T(8,128)S(1)} %collective-permute-done.5) | copy-start | bytes 2359300
  31.8 46.5 %collective-permute-start.7 = (f32[3,256,256]{2,1,0:T(8,128)S(1)}, f32[3,256,256]{2,1,0:T(8,128)}, u32[]{:S(2)}, u32[]{:S(2)}) collective-permute-start(f32[3,256,256]{2,1,0:T(8,128)S(1)} %collective-permute-done.5), channel_id=1, source_target_pairs={{0,6},{1,7},{8,14},{9,15},{16,22},{17,23},{24,30},{25,31},{32,38},... | collective-permute-start | bytes 2359304 | tf_op jit(solution)/shard_map/ppermute | solution.py:329
  33.1 45.3 %collective-permute-start.6 = (f32[3,256,256]{2,1,0:T(8,128)S(1)}, f32[3,256,256]{2,1,0:T(8,128)}, u32[]{:S(2)}, u32[]{:S(2)}) collective-permute-start(f32[3,256,256]{2,1,0:T(8,128)S(1)} %collective-permute-done.5), channel_id=1, source_target_pairs={{0,2},{1,3},{8,10},{9,11},{16,18},{17,19},{24,26},{25,27},{32,34},... | collective-permute-start | bytes 2359304 | tf_op jit(solution)/shard_map/ppermute | solution.py:328
  34.7 56.3 %copy-start.2 = (f32[3,256,256]{2,1,0:T(8,128)}, f32[3,256,256]{2,1,0:T(8,128)S(1)}, u32[]{:S(2)}) copy-start(f32[3,256,256]{2,1,0:T(8,128)S(1)} %collective-permute-done) | copy-start | bytes 2359300
  34.7 43.9 %collective-permute-start.2 = (f32[3,256,256]{2,1,0:T(8,128)S(1)}, f32[3,256,256]{2,1,0:T(8,128)}, u32[]{:S(2)}, u32[]{:S(2)}) collective-permute-start(f32[3,256,256]{2,1,0:T(8,128)S(1)} %collective-permute-done), channel_id=1, source_target_pairs={{2,4},{3,5},{10,12},{11,13},{18,20},{19,21},{26,28},{27,29},{34,36... | collective-permute-start | bytes 2359304 | tf_op jit(solution)/shard_map/ppermute | solution.py:330
  55.2 23.3 %all-to-all-start.2 = ((f32[32,3,8,256]{3,2,1,0:T(8,128)}), f32[32,3,8,256]{3,2,1,0:T(8,128)S(1)}, u32[]{:S(2)}, u32[]{:S(2)}) async-start(f32[32,3,8,256]{3,2,1,0:T(8,128)} %broadcast_in_dim.26), calls=%async_computation.2 | async-start | bytes 1572864 | tf_op jit(solution)/shard_map/all_to_all | solution.py:331
  79.4 31.1 %all-to-all-start.3 = ((f32[8,2,32,256]{3,2,1,0:T(8,128)}), f32[8,2,32,256]{3,2,1,0:T(8,128)S(1)}, u32[]{:S(2)}, u32[]{:S(2)}) async-start(f32[8,2,32,256]{3,2,1,0:T(8,128)} %broadcast_in_dim.24), calls=%async_computation.3 | async-start | bytes 1048576 | tf_op jit(solution)/shard_map/all_to_all | solution.py:338
  86.6 29.5 %collective-permute-start.8 = (f32[3,256,256]{2,1,0:T(8,128)}, f32[3,256,256]{2,1,0:T(8,128)}, u32[]{:S(2)}, u32[]{:S(2)}) collective-permute-start(f32[3,256,256]{2,1,0:T(8,128)} %collective-permute-done.7), channel_id=1, source_target_pairs={{6,4},{7,5},{14,12},{15,13},{22,20},{23,21},{30,28},{31,29},{38,36... | collective-permute-start | bytes 2359304 | tf_op jit(solution)/shard_map/ppermute | solution.py:335
  112.6 18.6 %all-to-all-start.4 = ((bf16[4,256,512]{2,1,0:T(8,128)(2,1)}), bf16[4,256,512]{2,1,0:T(8,128)(2,1)S(1)}, u32[]{:S(2)}, u32[]{:S(2)}) async-start(bf16[4,256,512]{2,1,0:T(8,128)(2,1)} %right_rows.1), calls=%async_computation.4 | async-start | bytes 2097152 | tf_op jit(solution)/shard_map/all_to_all | solution.py:343
  124.1 7.0 %collective-permute-start.10 = (f32[3,256,256]{2,1,0:T(8,128)}, f32[3,256,256]{2,1,0:T(8,128)S(1)}, u32[]{:S(2)}, u32[]{:S(2)}) collective-permute-start(f32[3,256,256]{2,1,0:T(8,128)} %get-tuple-element.28), channel_id=1, source_target_pairs={{0,1},{1,0},{8,9},{9,8},{16,17},{17,16},{24,25},{25,24},{32,33},{3... | collective-permute-start | bytes 2359304 | tf_op jit(solution)/shard_map/ppermute | solution.py:352
  124.8 6.3 %collective-permute-start.9 = (bf16[3,256,512]{2,1,0:T(8,128)(2,1)}, bf16[3,256,512]{2,1,0:T(8,128)(2,1)S(1)}, u32[]{:S(2)}, u32[]{:S(2)}) collective-permute-start(bf16[3,256,512]{2,1,0:T(8,128)(2,1)} %get-tuple-element.26.both_mine), channel_id=1, source_target_pairs={{0,1},{1,0},{2,3},{3,2},{4,5},{5,4},{6,7},{7,6},{8,9},{9,8},{10,11... | collective-permute-start | bytes 2359304 | tf_op jit(solution)/shard_map/ppermute | solution.py:351
